TPU v7x, 128 devices: a whole 4x4x4 slice. The times are simulated.
128 devices in a mesh: dp: 32 (over z_lo, x, y), tensor: 4 (over z_hi, core).
Axes of the slice: x: 4, y: 4, z: 4 (z_hi: 2, z_lo: 2; z = z_hi * 2 + z_lo), core: 2. Of those that a mesh axis runs over, the one named last changes fastest.
Arguments:
- hidden_in: bfloat16 [16384, 2048], P('dp'), may hold values from -6 to 6
- segment_ids: int32 [16384], P('dp'), may hold values from 0 to 3, as said below
- positions: int32 [16384], P('dp'), may hold values from 0 to 508, as said below
- ln1_gain: float32 [2048], replicated, may hold values from 0.1 to 1.9
- ln1_bias: float32 [2048], replicated, may hold values from -3 to 3
- qkv_weight: bfloat16 [2048, 6144], P(None, 'tensor'), may hold values from -0.125 to 0.125
- qkv_bias: float32 [8, 768], P('tensor'), may hold values from -3 to 3
- dense_weight: bfloat16 [2048, 2048], P('tensor'), may hold values from -0.5 to 0.5
- dense_bias: float32 [2048], replicated, may hold values from -3 to 3
- ln2_gain: float32 [2048], replicated, may hold values from 0.1 to 1.9
- ln2_bias: float32 [2048], replicated, may hold values from -3 to 3
- fc1_weight: bfloat16 [2048, 8192], P(None, 'tensor'), may hold values from -0.125 to 0.125
- fc1_bias: float32 [64, 128], P('tensor'), may hold values from -3 to 3
- fc2_weight: bfloat16 [8192, 2048], P('tensor'), may hold values from -0.0625 to 0.0625
- fc2_bias: float32 [2048], replicated, may hold values from -3 to 3
- cotangent: bfloat16 [16384, 2048], P('dp'), may hold values from -6 to 6
Outputs:
- output: float32 [16384, 2048], P('dp')
- input_grad: float32 [16384, 2048], P('dp')
- ln1_gain_grad: float32 [2048], P('dp')
- ln1_bias_grad: float32 [2048], P('dp')
- qkv_weight_grad: float32 [2048, 6144], P('dp', 'tensor')
- qkv_bias_grad: float32 [8, 768], P('tensor', 'dp')
- dense_weight_grad: float32 [2048, 2048], P('tensor', 'dp')
- dense_bias_grad: float32 [2048], P('dp')
- ln2_gain_grad: float32 [2048], P('dp')
- ln2_bias_grad: float32 [2048], P('dp')
- fc1_weight_grad: float32 [2048, 8192], P('dp', 'tensor')
- fc1_bias_grad: float32 [64, 128], P('tensor', 'dp')
- fc2_weight_grad: float32 [8192, 2048], P('tensor', 'dp')
- fc2_bias_grad: float32 [2048], P('dp')
Inputs may be any that keep to these rules, and one draw needn't show every extreme that they name: `segment_ids`: within each sequence of 512 tokens the segment numbers start at 0, never fall, and take each of the 4 values. `positions`: A token's index in its sequence minus the index of its document's first token.
All inputs are finite; a program needn't handle non-finite values.
Results may differ from a plain program's by a relative error of at most 0.011.
Values sent between devices are 32-bit elements; how exact they have to be, the bound alone decides.
No kernel may reach another device: no remote copies, remote signals or barrier semaphores. Data moves between devices by JAX's collectives and lax.ppermute only.
A program may use at most 256 MiB of HBM per device.

v0:
```python
from functools import partial
import math

import jax
import jax.numpy as jnp
import numpy as np
from jax import lax
from jax.experimental import pallas as pl
from jax.experimental.pallas import tpu as pltpu
from jax.sharding import Mesh, PartitionSpec as P

HD = 256
ROT = 64
TOK = 512
D = 2048
EPSILON = 1e-05
NEGATIVE = -1000000000.0
SIZES = {"zl": 2, "x": 4, "y": 4, "zh": 2, "c": 2}
DP = ("zl", "x", "y")
TENSOR = ("zh", "c")
F32 = jnp.float32
BF16 = jnp.bfloat16


def send(value, axis, step=1):
    n = SIZES[axis]
    return lax.ppermute(value, axis, [(i, (i + step) % n) for i in range(n)])


def swap(value, axis, bit):
    return lax.ppermute(value, axis, [(i, i ^ bit) for i in range(SIZES[axis])])


def plain_dot(left, right):
    return jnp.dot(left, right, preferred_element_type=F32)


def contract_cols(left, right):
    return lax.dot_general(left, right, (((1,), (1,)), ((), ())), preferred_element_type=F32)


VMEM = 56 * 1024 * 1024
VMEM_LESS = 24 * 1024 * 1024
WHOLE = 896
COST = pl.CostEstimate(flops=1000000, bytes_accessed=1000000, transcendentals=0)


def whole(shape):
    return pl.BlockSpec(shape, lambda *_: (0,) * len(shape), pipeline_mode=pl.Buffered(1))


def put_turned(target, rows):
    for z in range(2):
        for pair in range(8):
            start = z * 1024 + pair * 128
            block = rows[:, start : start + 128].T.astype(BF16)
            target[2 * pair, z] = block[:64]
            target[2 * pair + 1, z] = block[64:]


def normalise(hidden):
    average = jnp.mean(hidden, axis=-1, keepdims=True)
    centred = hidden - average
    inv_std = lax.rsqrt(jnp.mean(centred * centred, axis=-1, keepdims=True) + EPSILON)
    return centred * inv_std, average, inv_std


def first_kernel(
    hidden,
    cot,
    gain,
    shift,
    gain_two,
    shift_two,
    first_out,
    first_turned,
    second_turned,
    cot_turned,
    stats,
):
    normed, average, inv_std = normalise(hidden[...].astype(F32))
    first = normed * gain[...] + shift[...]
    first_out[...] = first.astype(BF16)
    put_turned(first_turned, first)
    put_turned(second_turned, normed * gain_two[...] + shift_two[...])
    put_turned(cot_turned, cot[...].astype(F32))
    lane = lax.broadcasted_iota(jnp.int32, (normed.shape[0], 128), 1)
    stats[...] = jnp.where(lane < 64, average, inv_std)


def first_far_kernel(near, other, gain, shift, gain_two, shift_two, *refs):
    first_out, second_out, first_turned, second_turned = refs[2:]

    def step(rows):
        normed, _, _ = normalise(rows)
        first = normed * gain[...] + shift[...]
        second = normed * gain_two[...] + shift_two[...]
        first_out[...] = first.astype(BF16)
        second_out[...] = second.astype(BF16)
        put_turned(first_turned, first)
        put_turned(second_turned, second)

    @pl.when(pl.program_id(0) < 2)
    def _():
        step(near[...])

    @pl.when(pl.program_id(0) >= 2)
    def _():
        step(other[...])


TURNED = (16, 2, 64, 2 * TOK)


def first(hidden, cot, params):
    rows = TOK // 2
    plain = pl.BlockSpec((rows, D), lambda i: (i, 0))
    return pl.pallas_call(
        first_kernel,
        grid=(2,),
        in_specs=[plain] * 2 + [whole((1, D))] * 4,
        out_specs=[plain]
        + [pl.BlockSpec((16, 2, 64, rows), lambda i: (0, 0, 0, i))] * 3
        + [pl.BlockSpec((rows, 128), lambda i: (i, 0))],
        out_shape=[jax.ShapeDtypeStruct((TOK, D), BF16)]
        + [jax.ShapeDtypeStruct(TURNED, BF16)] * 3
        + [jax.ShapeDtypeStruct((TOK, 128), F32)],
        compiler_params=pltpu.CompilerParams(vmem_limit_bytes=VMEM),
        cost_estimate=COST,
    )(hidden, cot, *(p.reshape(1, D) for p in params))


def first_far(near, other, params, held):
    rows = 128
    plain = pl.BlockSpec((rows, D), lambda i: (i, 0))
    return pl.pallas_call(
        first_far_kernel,
        grid=(TOK // rows,),
        in_specs=[
            pl.BlockSpec((rows, D), lambda i: (lax.min(i, 1), 0)),
            pl.BlockSpec((rows, D), lambda i: (lax.max(i - 2, 0), 0)),
        ]
        + [whole((1, D))] * 4
        + [pl.BlockSpec(memory_space=pl.ANY)] * 2,
        out_specs=[plain] * 2
        + [pl.BlockSpec((16, 2, 64, rows), lambda i: (0, 0, 0, i + TOK // rows))] * 2,
        out_shape=[jax.ShapeDtypeStruct((TOK, D), BF16)] * 2
        + [jax.ShapeDtypeStruct(TURNED, BF16)] * 2,
        input_output_aliases={6: 2, 7: 3},
        compiler_params=pltpu.CompilerParams(vmem_limit_bytes=VMEM),
        cost_estimate=COST,
    )(near, other, *(p.reshape(1, D) for p in params), *held)


def phi(upward):
    return 0.5 * (1.0 + lax.erf(upward * math.sqrt(0.5)))


def gelu_slope(upward, below):
    return below + upward * (jnp.exp(-0.5 * upward * upward) * (1.0 / math.sqrt(2.0 * math.pi)))


def as_row(block):
    return jnp.concatenate([block[i : i + 1, :] for i in range(block.shape[0])], axis=1)


def feed_kernel(hidden, gain, shift, cot, weight, bias, act_out, slope_out, down_grad, second):
    @pl.when(pl.program_id(0) == 0)
    def _():
        for start in (0, TOK // 2):
            rows = slice(start, start + TOK // 2)
            normed, _, _ = normalise(hidden[rows].astype(F32))
            second[rows] = (normed * gain[...] + shift[...]).astype(BF16)

    upward = plain_dot(second[...], weight[...]) + as_row(bias[0])
    below = phi(upward)
    act = (upward * below).astype(BF16)
    act_out[...] = act
    slope_out[...] = gelu_slope(upward, below)
    total = lax.dot_general(
        cot[...], act[:, :WHOLE], (((0,), (0,)), ((), ())), preferred_element_type=F32
    )
    for z in range(2):
        rows = total[z * 1024 : z * 1024 + 1024]
        down_grad[:, z * 64 : z * 64 + 64] = rows.reshape(16, 64, -1)


def feed(hidden, gain, shift, cot, weight, bias):
    units, width = weight.shape[1], 1024
    column = pl.BlockSpec((TOK, width), lambda j: (0, j))
    return pl.pallas_call(
        feed_kernel,
        grid=(units // width,),
        in_specs=[
            whole((TOK, D)),
            whole((1, D)),
            whole((1, D)),
            whole((TOK, D)),
            pl.BlockSpec((D, width), lambda j: (0, j)),
            pl.BlockSpec((1, width // 128, 128), lambda j: (j, 0, 0)),
        ],
        out_specs=[column, column, pl.BlockSpec((16, 128, WHOLE), lambda j: (0, 0, j))],
        out_shape=[
            jax.ShapeDtypeStruct((TOK, units), BF16),
            jax.ShapeDtypeStruct((TOK, units), F32),
            jax.ShapeDtypeStruct((16, 128, 2 * WHOLE), F32),
        ],
        scratch_shapes=[pltpu.VMEM((TOK, D), BF16)],
        compiler_params=pltpu.CompilerParams(vmem_limit_bytes=VMEM),
        cost_estimate=COST,
    )(
        hidden,
        gain.reshape(1, D),
        shift.reshape(1, D),
        cot,
        weight,
        bias.reshape(-1, width // 128, 128),
    )


def feed_back_kernel(cot, weight, slope, up_grad):
    up_grad[...] = (contract_cols(cot[...], weight[...]) * slope[...]).astype(BF16)


def feed_back(cot, weight, slope):
    units, width = slope.shape[1], 512
    column = pl.BlockSpec((TOK, width), lambda j: (0, j))
    return pl.pallas_call(
        feed_back_kernel,
        grid=(units // width,),
        in_specs=[whole((TOK, D)), pl.BlockSpec((width, D), lambda j: (j, 0)), column],
        out_specs=column,
        out_shape=jax.ShapeDtypeStruct((TOK, units), BF16),
        compiler_params=pltpu.CompilerParams(vmem_limit_bytes=VMEM),
        cost_estimate=COST,
    )(cot, weight, slope)


def cot_far_kernel(side, near, other, weight, slope, dense, held, up_grad, grad_mixed, cot_turned, low):
    half = TOK // 2

    @pl.when(pl.program_id(0) == 0)
    def _():
        for k, rows in enumerate((near, other)):
            low[k * half : k * half + half] = rows[...].astype(BF16)
            put_turned(cot_turned.at[:, :, :, k * half : k * half + half], rows[...])
        grad_mixed[...] = contract_cols(low[...], dense[...]).astype(BF16)

    up_grad[...] = (contract_cols(low[...], weight[...]) * slope[...]).astype(BF16)


def cot_far(side, near, other, weight, slope, dense, held):
    width = 256
    steps = slope.shape[1] // width
    column = pl.BlockSpec((TOK, width), lambda j, s: (0, j))
    return pl.pallas_call(
        cot_far_kernel,
        grid_spec=pltpu.PrefetchScalarGridSpec(
            num_scalar_prefetch=1,
            grid=(steps,),
            in_specs=[
                whole((TOK // 2, D)),
                whole((TOK // 2, D)),
                pl.BlockSpec((width, D), lambda j, s: (s[0] * steps + j, 0)),
                column,
                pl.BlockSpec((HD, D), lambda j, s: (s[0], 0)),
                pl.BlockSpec(memory_space=pl.ANY),
            ],
            out_specs=[
                column,
                pl.BlockSpec((TOK, HD), lambda j, s: (0, 0)),
                pl.BlockSpec((16, 2, 64, TOK), lambda j, s: (0, 0, 0, 1)),
            ],
            scratch_shapes=[pltpu.VMEM((TOK, D), BF16)],
        ),
        out_shape=[
            jax.ShapeDtypeStruct((TOK, slope.shape[1]), BF16),
            jax.ShapeDtypeStruct((TOK, HD), BF16),
            jax.ShapeDtypeStruct(TURNED, BF16),
        ],
        input_output_aliases={6: 2},
        compiler_params=pltpu.CompilerParams(vmem_limit_bytes=VMEM),
        cost_estimate=COST,
    )(side, near, other, weight, slope, dense, held)


def slope_far_kernel(side, second, weight, bias, slope, act_out):
    upward = plain_dot(second[...], weight[...]) + as_row(bias[0])
    below = phi(upward)
    slope[...] = gelu_slope(upward, below)

    @pl.when(pl.program_id(0) == pl.num_programs(0) - 1)
    def _():
        shared = act_out.shape[1]
        act_out[...] = (upward[:, -shared:] * below[:, -shared:]).astype(BF16)


def slope_far(side, second, weight, bias):
    units, width = weight.shape[1] // 2, 512
    steps = units // width
    return pl.pallas_call(
        slope_far_kernel,
        grid_spec=pltpu.PrefetchScalarGridSpec(
            num_scalar_prefetch=1,
            grid=(steps,),
            in_specs=[
                whole((TOK, D)),
                pl.BlockSpec((D, width), lambda j, s: (0, s[0] * steps + j)),
                pl.BlockSpec((1, width // 128, 128), lambda j, s: (s[0] * steps + j, 0, 0)),
            ],
            out_specs=[
                pl.BlockSpec((TOK, width), lambda j, s: (0, j)),
                pl.BlockSpec((TOK, units - WHOLE), lambda j, s: (0, 0)),
            ],
        ),
        out_shape=[
            jax.ShapeDtypeStruct((TOK, units), F32),
            jax.ShapeDtypeStruct((TOK, units - WHOLE), BF16),
        ],
        compiler_params=pltpu.CompilerParams(vmem_limit_bytes=VMEM),
        cost_estimate=COST,
    )(side, second, weight, bias.reshape(-1, width // 128, 128))


def turn(values, tables, sign):
    first = values[:, :128]
    cosine, rising, falling = tables
    first = (
        first * cosine[...]
        + (pltpu.roll(first, 32, 1) * rising[...] + pltpu.roll(first, 96, 1) * falling[...]) * sign
    )
    return jnp.concatenate([first, values[:, 128:]], axis=1)


def as_column(row):
    return jnp.broadcast_to(row, (8, row.shape[1])).T[:, 0:1]


def cosine_and_sine(angles):
    turns = jnp.floor(angles * (2.0 / math.pi) + 0.5)
    rest = ((angles - turns * 1.5703125) - turns * 4.837512969970703e-4) - turns * 7.549789954891882e-8
    square = rest * rest
    sine = ((-1.9515295891e-4 * square + 8.3321608736e-3) * square - 1.6666654611e-1) * square
    sine = sine * rest + rest
    cosine = (2.443315711809948e-5 * square - 1.388731625493765e-3) * square + 4.166664568298827e-2
    cosine = cosine * (square * square) - 0.5 * square + 1.0
    quarter = turns.astype(jnp.int32) & 3
    odd = (quarter & 1) == 1
    flipped = jnp.where(odd, sine, cosine), jnp.where(odd, cosine, sine)
    return (
        jnp.where((quarter == 1) | (quarter == 2), -flipped[0], flipped[0]),
        jnp.where(quarter >= 2, -flipped[1], flipped[1]),
    )


def project_kernel(place, first, weight, bias, marks, inverse, queries, keys, values, *tables):
    @pl.when(pl.program_id(0) == 0)
    def _():
        angles = inverse[...] * marks[1:2, :]
        cosine, sine = cosine_and_sine(angles)
        none, rest = jnp.zeros_like(sine), jnp.zeros((64, TOK), F32)
        tables[0][...] = jnp.concatenate([cosine, cosine, rest + 1.0], axis=0).T
        tables[1][...] = jnp.concatenate([none, sine, rest], axis=0).T
        tables[2][...] = jnp.concatenate([-sine, none, rest], axis=0).T

    head = pl.program_id(0) + place[0] * (2 - pl.num_programs(0))
    packed = plain_dot(first[...], weight[...]) + bias[pl.ds(head, 1), :]
    queries[...] = turn(packed[:, :HD], tables, 1.0).astype(BF16)
    keys[...] = turn(packed[:, HD : 2 * HD], tables, 1.0).astype(BF16)
    values[...] = packed[:, 2 * HD :].astype(BF16)


def project(place, heads, first, weight, bias, marks):
    inverse = jnp.asarray((10000.0 ** (-2.0 * np.arange(32) / ROT)).astype(np.float32).reshape(32, 1))
    at = (lambda h, s: h) if heads == 2 else (lambda h, s: s[0])
    column = pl.BlockSpec((TOK, HD), lambda h, s: (0, h))
    return pl.pallas_call(
        project_kernel,
        grid_spec=pltpu.PrefetchScalarGridSpec(
            num_scalar_prefetch=1,
            grid=(heads,),
            in_specs=[
                whole((TOK, D)),
                pl.BlockSpec((D, 3 * HD), lambda h, s: (0, at(h, s))),
                whole((2, 3 * HD)),
                whole((2, TOK)),
                whole((32, 1)),
            ],
            out_specs=[column] * 3 + [pl.BlockSpec((TOK, 128), lambda h, s: (0, 0))] * 3,
        ),
        out_shape=[jax.ShapeDtypeStruct((TOK, heads * HD), BF16)] * 3
        + [jax.ShapeDtypeStruct((TOK, 128), F32)] * 3,
        compiler_params=pltpu.CompilerParams(vmem_limit_bytes=VMEM),
        cost_estimate=COST,
    )(place, first, weight, bias, marks, inverse)


def attend_kernel(place, queries, keys, values, cosine, rising, falling, marks, *refs):
    given, (mixed_out, grad_out) = refs[:-2], refs[-2:]
    tables = (cosine, rising, falling)
    scale = 1.0 / math.sqrt(HD)
    queries, keys, values = queries[...], keys[...], values[...]
    segments = marks[0:1, :]

    def order(axis):
        return lax.rem(lax.broadcasted_iota(jnp.int32, (TOK, TOK), axis) + place[1], TOK)

    allowed = (as_column(segments) == segments) & (order(0) >= order(1))
    scores = jnp.where(allowed, contract_cols(queries, keys) * scale, NEGATIVE)
    top = jnp.max(scores, axis=-1, keepdims=True)
    weights = jnp.exp(scores - top)
    probs = weights / jnp.sum(weights, axis=-1, keepdims=True)
    probs_low = probs.astype(BF16)
    mixed_out[...] = plain_dot(probs_low, values).astype(BF16)
    grad_mixed = given[0][...]
    if len(given) == 2:
        grad_mixed = contract_cols(grad_mixed, given[1][...]).astype(BF16)
    grad_probs = contract_cols(grad_mixed, values)
    along = jnp.sum(probs * grad_probs, axis=-1, keepdims=True)
    grad_scores = (probs * (grad_probs - along)).astype(BF16)
    grad_query = plain_dot(grad_scores, keys) * scale
    grad_key = plain_dot(grad_scores.T, queries) * scale
    grad_value = plain_dot(probs_low.T, grad_mixed)
    grad_out[:, :HD] = turn(grad_query, tables, -1.0).astype(BF16)
    grad_out[:, HD : 2 * HD] = turn(grad_key, tables, -1.0).astype(BF16)
    grad_out[:, 2 * HD :] = grad_value.astype(BF16)


def attend(place, heads, projected, given, marks):
    column = pl.BlockSpec((TOK, HD), lambda h, s: (0, h))
    return pl.pallas_call(
        attend_kernel,
        grid_spec=pltpu.PrefetchScalarGridSpec(
            num_scalar_prefetch=1,
            grid=(heads,),
            in_specs=[column] * 3
            + [whole((TOK, 128))] * 3
            + [whole((2, TOK))]
            + ([column] if len(given) == 1 else [whole((TOK, D)), pl.BlockSpec((HD, D), lambda h, s: (h, 0))]),
            out_specs=[column, pl.BlockSpec((TOK, 3 * HD), lambda h, s: (0, h))],
        ),
        out_shape=[
            jax.ShapeDtypeStruct((TOK, heads * HD), BF16),
            jax.ShapeDtypeStruct((TOK, heads * 3 * HD), BF16),
        ],
        compiler_params=pltpu.CompilerParams(vmem_limit_bytes=VMEM),
        cost_estimate=COST,
    )(place, *projected, marks, *given)


def put_halves(core, values, scratch, mine, other):
    scratch[...] = values
    half = TOK // 2
    mine[...] = scratch[pl.ds(pl.multiple_of(core[0] * half, half), half), :]
    other[...] = scratch[pl.ds(pl.multiple_of((1 - core[0]) * half, half), half), :]


def branch_kernel(mixed, act, dense, down, total):
    total[...] = plain_dot(act[...], down[...]) + plain_dot(mixed[...], dense[...])


def back_kernel(
    core, packed, up_grad, qkv, up, hidden, stats, gain, gain_two, mine, other, sums, scratch
):
    first = contract_cols(packed[...], qkv[...])
    second = contract_cols(up_grad[...], up[...])
    put_halves(core, first * gain[...] + second * gain_two[...], scratch, mine, other)
    normed = (hidden[...].astype(F32) - stats[:, 0:1]) * stats[:, 64:65]
    rows = [
        jnp.sum(v, axis=0, keepdims=True) for v in (first * normed, first, second * normed, second)
    ]
    sums[...] = jnp.concatenate(rows + [jnp.zeros((4, first.shape[1]), F32)], axis=0)


def halves_call(kernel, core, operands, specs, with_sums):
    width = 512
    half = pl.BlockSpec((TOK // 2, width), lambda j, s: (0, j))
    return pl.pallas_call(
        kernel,
        grid_spec=pltpu.PrefetchScalarGridSpec(
            num_scalar_prefetch=1,
            grid=(D // width,),
            in_specs=specs,
            out_specs=[half, half] + [pl.BlockSpec((8, width), lambda j, s: (0, j))] * with_sums,
            scratch_shapes=[pltpu.VMEM((TOK, width), F32)],
        ),
        out_shape=[jax.ShapeDtypeStruct((TOK // 2, D), F32)] * 2
        + [jax.ShapeDtypeStruct((8, D), F32)] * with_sums,
        compiler_params=pltpu.CompilerParams(vmem_limit_bytes=VMEM),
        cost_estimate=COST,
    )(core, *operands)


def branches(mixed, act, dense, down):
    width = 512
    return pl.pallas_call(
        branch_kernel,
        grid=(D // width,),
        in_specs=[whole(mixed.shape), whole(act.shape)]
        + [pl.BlockSpec((w.shape[0], width), lambda j: (0, j)) for w in (dense, down)],
        out_specs=pl.BlockSpec((TOK, width), lambda j: (0, j)),
        out_shape=jax.ShapeDtypeStruct((TOK, D), F32),
        compiler_params=pltpu.CompilerParams(vmem_limit_bytes=VMEM),
        cost_estimate=COST,
    )(mixed, act, dense, down)


def back_halves(core, packed, up_grad, qkv, up, hidden, stats, gain, gain_two):
    specs = [whole(packed.shape), whole(up_grad.shape)]
    specs += [pl.BlockSpec((512, w.shape[1]), lambda j, s: (j, 0)) for w in (qkv, up)]
    specs += [pl.BlockSpec((TOK, 512), lambda j, s: (0, j)), whole((TOK, 128))]
    specs += [pl.BlockSpec((1, 512), lambda j, s: (0, j))] * 2
    operands = (packed, up_grad, qkv, up, hidden, stats, gain.reshape(1, D), gain_two.reshape(1, D))
    return halves_call(back_kernel, core, operands, specs, True)


def final_kernel(n, half, branch, combined, hidden, cot, stats, bias, bias_too, *refs):
    output, input_grad = refs[n:]
    rows = hidden[...].astype(F32)
    output[...] = rows + branch[...] + bias[...] + bias_too[...]
    e = combined[...]
    inv_std = stats[:, 64:65]
    normed = (rows - stats[:, 0:1]) * inv_std
    input_grad[...] = cot[...].astype(F32) + inv_std * (
        e
        - jnp.mean(e, axis=-1, keepdims=True)
        - normed * jnp.mean(e * normed, axis=-1, keepdims=True)
    )


def final_half(half, branch, combined, hidden, cot, stats, biases, held):
    rows = 128
    steps = TOK // 2 // rows
    given = pl.BlockSpec((rows, D), lambda i, s: (i, 0))
    placed = pl.BlockSpec((rows, D), lambda i, s: (s[0] * steps + i, 0))
    return pl.pallas_call(
        partial(final_kernel, len(held)),
        grid_spec=pltpu.PrefetchScalarGridSpec(
            num_scalar_prefetch=1,
            grid=(steps,),
            in_specs=[placed, given, placed, placed]
            + [pl.BlockSpec((rows, 128), lambda i, s: (s[0] * steps + i, 0))]
            + [whole((1, D))] * 2
            + [pl.BlockSpec(memory_space=pl.ANY)] * len(held),
            out_specs=[placed, placed],
        ),
        out_shape=[jax.ShapeDtypeStruct((TOK, D), F32)] * 2,
        input_output_aliases={8: 0, 9: 1} if held else {},
        compiler_params=pltpu.CompilerParams(vmem_limit_bytes=VMEM_LESS),
        cost_estimate=COST,
    )(half, branch, combined, hidden, cot, stats, *(b.reshape(1, D) for b in biases), *held)


def joint_kernel(side, *refs):
    lefts, rights, target, held, right, arrived = (
        refs[:3],
        refs[3:11],
        refs[11],
        refs[12],
        refs[13],
        refs[14],
    )
    step = pl.program_id(0)
    copies = [pltpu.make_async_copy(lefts[k], held.at[k], arrived.at[k]) for k in range(3)]

    @pl.when(step == 0)
    def _():
        for copy in copies:
            copy.start()
        copies[0].wait()

    @pl.when(step == 4)
    def _():
        copies[1].wait()
        copies[2].wait()

    for n, (start, stop) in enumerate(((0, 4), (4, 5), (5, 8), (8, 9))):

        @pl.when((step >= start) & (step < stop))
        def _(n=n):
            for k in range(2):
                given = rights[2 * n + k]
                right[k * TOK : k * TOK + TOK, : given.shape[1]] = given[...]

    k = jnp.where(step < 4, 0, jnp.where((step >= 5) & (step < 8), 2, 1))
    target[...] = plain_dot(held[k].reshape(D, 2 * TOK), right[...]).reshape(16, 128, -1)


def joint(side, lefts, rights):
    width, shared = 256, 1024 - WHOLE
    specs = [pl.BlockSpec(memory_space=pl.ANY)] * 3
    for start, n in ((0, 4), (4, 1), (5, 3)):

        def near(j, s, start=start, n=n):
            return (0, s[0] * n + jnp.clip(j - start, 0, n - 1))

        def far(j, s, start=start, n=n):
            return (0, jnp.clip(j - start, 0, n - 1))

        specs += [pl.BlockSpec((TOK, width), near), pl.BlockSpec((TOK, width), far)]
    specs += [
        pl.BlockSpec((TOK, shared), lambda j, s: (0, (s[0] + 1) * (1024 // shared) - 1)),
        pl.BlockSpec((TOK, shared), lambda j, s: (0, 0)),
    ]
    return pl.pallas_call(
        joint_kernel,
        grid_spec=pltpu.PrefetchScalarGridSpec(
            num_scalar_prefetch=1,
            grid=(9,),
            in_specs=specs,
            out_specs=pl.BlockSpec((16, 128, width), lambda j, s: (0, 0, j)),
            scratch_shapes=[
                pltpu.VMEM((3,) + TURNED, BF16),
                pltpu.VMEM((2 * TOK, width), BF16),
                pltpu.SemaphoreType.DMA((3,)),
            ],
        ),
        out_shape=jax.ShapeDtypeStruct((16, 128, 2048 + shared), F32),
        compiler_params=pltpu.CompilerParams(vmem_limit_bytes=VMEM),
        cost_estimate=COST,
    )(side, *lefts, *rights)


def assemble_kernel(side, near, far, part, up, dense, qkv, down):
    def put(low, high):
        up[...] = jnp.concatenate([low[:, :1024], high[:, :1024]], axis=1)
        dense[...] = jnp.concatenate([low[:, 1024:1280], high[:, 1024:1280]], axis=1)
        qkv[...] = jnp.concatenate([low[:, 1280:2048], high[:, 1280:2048]], axis=1)
        down[...] = jnp.concatenate(
            [part[:, :WHOLE], low[:, 2048:], part[:, WHOLE:], high[:, 2048:]], axis=1
        )

    @pl.when(side[0] == 0)
    def _():
        put(near[0], far[...])

    @pl.when(side[0] != 0)
    def _():
        put(far[...], near[0])


def assemble(side, near, far, part):
    shapes = ((64, 2048), (64, 512), (64, 1536), (64, 2048))
    columns = far.shape[1]
    return pl.pallas_call(
        assemble_kernel,
        grid_spec=pltpu.PrefetchScalarGridSpec(
            num_scalar_prefetch=1,
            grid=(1,),
            in_specs=[
                pl.BlockSpec((1, 64, columns), lambda i, s: (0, s[0], 0)),
                pl.BlockSpec((64, columns), lambda i, s: (0, 0)),
                pl.BlockSpec((64, 2 * WHOLE), lambda i, s: (0, 0)),
            ],
            out_specs=[pl.BlockSpec(shape, lambda i, s: (0, 0)) for shape in shapes],
        ),
        out_shape=[jax.ShapeDtypeStruct(shape, F32) for shape in shapes],
        compiler_params=pltpu.CompilerParams(vmem_limit_bytes=VMEM_LESS),
        cost_estimate=COST,
    )(side, near, far, part)


def body(
    hidden_in,
    segment_ids,
    positions,
    ln1_gain,
    ln1_bias,
    qkv_weight,
    qkv_bias,
    dense_weight,
    dense_bias,
    ln2_gain,
    ln2_bias,
    fc1_weight,
    fc1_bias,
    fc2_weight,
    fc2_bias,
    cotangent,
):
    core = lax.axis_index("c")
    side = lax.axis_index("zl")
    half_rows = TOK // 2
    at_side = side.astype(jnp.int32).reshape(1)
    at_core = core.astype(jnp.int32).reshape(1)
    own_place = jnp.zeros((2,), jnp.int32)
    far_place = jnp.stack([side, core * half_rows]).astype(jnp.int32)
    after = lax.optimization_barrier
    params = (ln1_gain, ln1_bias, ln2_gain, ln2_bias)

    def of_core(values, which):
        return lax.dynamic_slice_in_dim(values, which * half_rows, half_rows, 0)

    act_low, slope, down_grad = feed(
        hidden_in, ln2_gain, ln2_bias, cotangent, fc1_weight, fc1_bias
    )
    down_sum = after(lax.psum_scatter(down_grad, ("x", "y"), scatter_dimension=0, tiled=True))
    _, cotangent, hidden_in = after((down_grad, cotangent, hidden_in))

    hidden_got = send(of_core(hidden_in, core).astype(F32), "zl")
    marks = jnp.concatenate([segment_ids, positions]).astype(F32).reshape(1, 2 * TOK)
    cot_sent = jnp.concatenate(
        [of_core(cotangent, core).astype(F32), jnp.pad(marks, ((0, 7), (0, D - 2 * TOK)))], axis=0
    )
    cot_got = lax.ppermute(cot_sent, ("zl", "zh"), [(i, 3 - i) for i in range(4)])

    own_marks = marks.reshape(2, TOK)

    def own_step(hidden_in, cotangent, act_low, slope):
        first_in, *turned, stats = first(hidden_in, cotangent, params)
        projected = project(own_place, 2, first_in, qkv_weight, qkv_bias, own_marks)
        mixed_low, grad_packed = attend(
            own_place, 2, projected, (cotangent, dense_weight), own_marks
        )
        grad_up = feed_back(cotangent, fc2_weight, slope)
        branch = branches(mixed_low, act_low, dense_weight, fc2_weight)
        return *turned, stats, mixed_low, grad_packed, grad_up, branch

    (
        first_turned,
        second_turned,
        cot_turned,
        stats,
        mixed_low,
        grad_packed,
        grad_up,
        branch,
    ) = lax.cond(core > 1, own_step, own_step, hidden_in, cotangent, act_low, slope)
    branch = lax.psum(branch, TENSOR)
    hidden_got, mixed_low = after((hidden_got, mixed_low))
    hidden_too = send(hidden_got, "c")
    hidden_too, cot_got = after((hidden_too, cot_got))
    cot_too = send(cot_got, "c")

    first_far_in, second_far_in, first_turned, second_turned = first_far(
        hidden_got, hidden_too, params, (first_turned, second_turned)
    )
    slope_side, act_far = slope_far(at_side, second_far_in, fc1_weight, fc1_bias)
    marks_got = cot_got[half_rows, : 2 * TOK].reshape(2, 2, half_rows)
    marks_far = jnp.where(core == 0, marks_got, marks_got[:, ::-1]).reshape(2, TOK)
    projected_far = project(far_place, 1, first_far_in, qkv_weight, qkv_bias, marks_far)
    grad_up_far, grad_mixed_far, cot_turned = cot_far(
        at_side, cot_got, cot_too, fc2_weight, slope_side, dense_weight, cot_turned
    )
    mixed_far, grad_packed_far = attend(
        far_place, 1, projected_far, (grad_mixed_far,), marks_far
    )
    joint_grad = joint(
        at_side,
        (second_turned, cot_turned, first_turned),
        (
            grad_up,
            grad_up_far,
            mixed_low,
            mixed_far,
            grad_packed,
            grad_packed_far,
            act_low,
            act_far,
        ),
    )
    joint_grad, down_sum = after((joint_grad, down_sum))
    joint_sum = after(lax.psum_scatter(joint_grad, ("x", "y"), scatter_dimension=0, tiled=True))
    _, grad_packed, grad_up, cotangent, down_sum = after(
        (joint_grad, grad_packed, grad_up, cotangent, down_sum)
    )

    combined, combined_other, norms = back_halves(
        at_core, grad_packed, grad_up, qkv_weight, fc1_weight, hidden_in, stats, ln1_gain, ln2_gain
    )
    combined = combined + send(combined_other, "c")
    combined_too = send(combined, "zh")

    norms = norms[:4].reshape(4, 32, 64).transpose(1, 0, 2).reshape(32, 256)
    grad_out = cotangent.astype(F32)
    bias_sum = jnp.sum(grad_out, axis=0)
    qkv_bias_sum = jnp.sum(grad_packed.astype(F32), axis=0)
    up_bias_grad = jnp.sum(grad_up.astype(F32), axis=0)
    small = jnp.concatenate(
        [
            norms,
            bias_sum.reshape(32, 64),
            qkv_bias_sum.reshape(2, 32, 24).transpose(1, 0, 2).reshape(32, 48),
            up_bias_grad.reshape(16, 32, 4).transpose(1, 0, 2).reshape(32, 64),
            jnp.zeros((32, 80), F32),
        ],
        axis=1,
    )
    def of_side(values, which):
        return lax.dynamic_slice_in_dim(values[0], which * 64, 64, 0)

    down_far = send(of_side(down_sum, 1 - side), "zl")
    for axis in ("x", "y"):
        small = small + swap(small, axis, 1)
        small = small + swap(small, axis, 2)
    block = lax.axis_index("x") * 4 + lax.axis_index("y")
    own_small = lax.dynamic_slice_in_dim(small, side * 16 + block, 1, 0)
    far_small = lax.dynamic_slice_in_dim(small, (1 - side) * 16 + block, 1, 0)
    small = (own_small + send(far_small, "zl")).reshape(-1)

    norms = small[:256]
    norms = norms + send(norms, "c")
    norms = norms + send(norms, "zh")
    norms, branch, combined_too, down_far = after((norms, branch, combined_too, down_far))
    combined = combined + combined_too
    norms = norms.reshape(4, 64)
    bias_total = small[256:320]
    biases = (dense_bias, fc2_bias)
    own = (hidden_in, cotangent, stats, biases)
    combined_too = send(combined, "c")
    finals = final_half(at_core, branch, combined, *own, ())
    finals = final_half(1 - at_core, branch, combined_too, *own, finals)
    output, input_grad, joint_sum = after((*finals, joint_sum))

    down_sum = of_side(down_sum, side) + down_far
    joint_far = send(of_side(joint_sum, 1 - side), "zl")
    up_sum, dense_sum, qkv_sum, down_sum = assemble(at_side, joint_sum, joint_far, down_sum)
    return (
        output,
        input_grad,
        norms[0],
        norms[1],
        qkv_sum,
        small[320:368].reshape(2, 24),
        dense_sum.T,
        bias_total,
        norms[2],
        norms[3],
        up_sum,
        small[368:432].reshape(16, 4),
        down_sum.T,
        bias_total,
    )


def solution(mesh):
    fine = Mesh(mesh.devices.reshape(tuple(SIZES.values())), tuple(SIZES))
    return jax.shard_map(
        body,
        mesh=fine,
        in_specs=(
            P(DP, None),
            P(DP),
            P(DP),
            P(),
            P(),
            P(None, TENSOR),
            P(TENSOR, None),
            P(TENSOR, None),
            P(),
            P(),
            P(),
            P(None, TENSOR),
            P(TENSOR, None),
            P(TENSOR, None),
            P(),
            P(DP, None),
        ),
        out_specs=(
            P(DP, None),
            P(DP, None),
            P(DP),
            P(DP),
            P(DP, TENSOR),
            P(TENSOR, DP),
            P(TENSOR, DP),
            P(DP),
            P(DP),
            P(DP),
            P(DP, TENSOR),
            P(TENSOR, DP),
            P(TENSOR, DP),
            P(DP),
        ),
        check_vma=False,
    )
```

profile of v0, /device:TPU:0, one launch (start us, length us, event | category | flops | bytes accessed | tf_op | source)
XLA Modules:
  0.0 281.9 jit_solution(14862228319943669519)
XLA Ops:
  8.1 17.6 %shard_map.281 = (bf16[512,2048]{1,0:T(8,128)(2,1)}, f32[512,2048]{1,0:T(8,128)}, f32[16,128,1792]{2,1,0:T(8,128)}) custom-call(bf16[512,2048]{1,0:T(8,128)(2,1)} %hidden.4, f32[1,2048]{1,0:T(1,128)} %bitcast.47, f32[1,2048]{1,0:T(1,128)} %bitcast.58, bf16[512,2048]{1,0:T(8,128)(2,1)} %cot.3, bf16[2048,2048]{1,0:T(8,128)(2,1)} %up.1, f32[2,8,128]{2,1,0:T(8,128)} %bitcast.68), custom_call_target="tpu_custom_call" | custom-call | flops 1000000 | bytes 1000000 | tf_op jit(solution)/shard_map/pallas_call | solution.py:191
  25.7 2.9 %dynamic-slice_convert_fusion.1 = f32[256,2048]{1,0:T(8,128)} fusion(bf16[512,2048]{1,0:T(8,128)(2,1)} %hidden.4, s32[]{:T(128)S(6)} %select_n.25), kind=kLoop, calls=%fused_computation.6 | loop fusion | flops 524288 | bytes 3145732 | tf_op jit(solution)/shard_map/convert_element_type | solution.py:700
  32.5 2.5 collective-permute-start.2
  35.1 41.6 %conditional.1 = (bf16[16,2,64,1024]{3,2,1,0:T(8,128)(2,1)}, bf16[16,2,64,1024]{3,2,1,0:T(8,128)(2,1)}, bf16[16,2,64,1024]{3,2,1,0:T(8,128)(2,1)}, f32[512,128]{...) conditional(s32[]{:T(128)} %convert_element_type.37, ...), branch_computations={%region_0.0_spmd, %region_1.2_spmd} | conditional | flops 5000000 | bytes 30165984 | solution.py:728
  35.1 9.1 %branch_0_fun.8 = bf16[512,2048]{1,0:T(8,128)(2,1)} custom-call(bf16[512,2048]{1,0:T(8,128)(2,1)S(1)} %get-tuple-element.57.cot.refs_0_, bf16[2048,2048]{1,0:T(8,128)(2,1)} %get-tuple-element.80.weight.down, f32[512,2048]{1,0:T(8,128)} %get-tuple-element.81.slope), custom_call_target="tpu_custom_call" | custom-call | flops 1000000 | bytes 1000000 | tf_op jit(solution)/shard_map/cond/branch_0_fun/pallas_call | solution.py:228
  44.3 5.0 %branch_0_fun.5 = (bf16[512,2048]{1,0:T(8,128)(2,1)}, bf16[16,2,64,1024]{3,2,1,0:T(8,128)(2,1)}, bf16[16,2,64,1024]{3,2,1,0:T(8,128)(2,1)}, bf16[16,2,64,1024]{3,2,1,0:T(8,128)(2,1)}, f32[512,128]{1,0:T(8,128)S(1)}) custom-call(bf16[512,2048]{1,0:T(8,128)(2,1)S(1)} %copy-done.8, bf16[512,2048]{1,0:T(8,128)(2,1)S(1)} %get-tuple-element.57.cot.refs_0_, ...), custom_call_target="tpu_custom_call" | custom-call | flops 1000000 | bytes 1000000 | tf_op jit(solution)/shard_map/cond/branch_0_fun/pallas_call | solution.py:118
  49.8 8.5 %branch_0_fun.6 = (bf16[512,512]{1,0:T(8,128)(2,1)}, bf16[512,512]{1,0:T(8,128)(2,1)}, bf16[512,512]{1,0:T(8,128)(2,1)}, f32[512,128]{1,0:T(8,128)}, f32[512,128]{1,0:T(8,128)}, /*index=5*/f32[512,128]{1,0:T(8,128)}) custom-call(s32[2]{0:T(128)} %broadcast_1_place.0.place, bf16[512,2048]{1,0:T(8,128)(2,1)} %get-tuple-element.66.first, ...), custom_call_target="tpu_custom_call" | custom-call | flops 1000000 | bytes 1000000 | tf_op jit(solution)/shard_map/cond/branch_0_fun/pallas_call | solution.py:377
  58.3 8.8 %branch_0_fun.7 = (bf16[512,512]{1,0:T(8,128)(2,1)}, bf16[512,1536]{1,0:T(8,128)(2,1)}) custom-call(s32[2]{0:T(128)} %broadcast_1_place.0.place, bf16[512,512]{1,0:T(8,128)(2,1)} %get-tuple-element.71.queries, bf16[512,512]{1,0:T(8,128)(2,1)} %get-tuple-element.72.keys, bf16[512,512]{1,0:T(8,128)(2,1)} %get-tuple-element.73.values, ...), custom_call_target="tpu_custom_call" | custom-call | flops 1000000 | bytes 1000000 | tf_op jit(solution)/shard_map/cond/branch_0_fun/pallas_call | solution.py:431
  67.1 9.6 %branch_0_fun.9 = f32[512,2048]{1,0:T(8,128)} custom-call(bf16[512,512]{1,0:T(8,128)(2,1)} %get-tuple-element.294.mixed, bf16[512,2048]{1,0:T(8,128)(2,1)S(1)} %copy-done.14, bf16[512,2048]{1,0:T(8,128)(2,1)S(1)} %copy-done.11, bf16[2048,2048]{1,0:T(8,128)(2,1)} %get-tuple-element.80.weight.down), custom_call_target="tpu_custom_call" | custom-call | flops 1000000 | bytes 1000000 | tf_op jit(solution)/shard_map/cond/branch_0_fun/pallas_call | solution.py:496
  76.9 5.7 %collective-permute-done.2.near = f32[264,2048]{1,0:T(8,128)} collective-permute-done((f32[264,2048]{1,0:T(8,128)}, f32[264,2048]{1,0:T(8,128)}, u32[]{:S(2)}, u32[]{:S(2)}) %collective-permute-start.2) | collective-permute-done | bytes 2162720 | tf_op jit(solution)/shard_map/ppermute | solution.py:705
  84.6 7.9 %shard_map.282 = (bf16[512,2048]{1,0:T(8,128)(2,1)}, bf16[512,2048]{1,0:T(8,128)(2,1)}, bf16[16,2,64,1024]{3,2,1,0:T(8,128)(2,1)}, bf16[16,2,64,1024]{3,2,1,0:T(8,128)(2,1)}) custom-call(f32[256,2048]{1,0:T(8,128)} %collective-permute-done.near, f32[256,2048]{1,0:T(8,128)} %collective-permute-done.1.other, ...), custom_call_target="tpu_custom_call", output_to_operand_aliasing={{2}: (6, {}), {3}: (7, {})} | custom-call | flops 1000000 | bytes 1000000 | tf_op jit(solution)/shard_map/pallas_call | solution.py:136
  92.5 6.5 %shard_map.283 = (f32[512,1024]{1,0:T(8,128)}, bf16[512,128]{1,0:T(8,128)(2,1)}) custom-call(s32[1]{0:T(128)} %bitcast.9.side, bf16[512,2048]{1,0:T(8,128)(2,1)} %get-tuple-element.194.second, bf16[2048,2048]{1,0:T(8,128)(2,1)} %up.1, f32[4,4,128]{2,1,0:T(4,128)} %bitcast.69), custom_call_target="tpu_custom_call" | custom-call | flops 1000000 | bytes 1000000 | tf_op jit(solution)/shard_map/pallas_call | solution.py:301
  99.0 6.2 %shard_map.285 = (bf16[512,256]{1,0:T(8,128)(2,1)}, bf16[512,256]{1,0:T(8,128)(2,1)}, bf16[512,256]{1,0:T(8,128)(2,1)}, f32[512,128]{1,0:T(8,128)}, f32[512,128]{1,0:T(8,128)}, /*index=5*/f32[512,128]{1,0:T(8,128)}) custom-call(s32[2]{0:T(128)} %pad_add_fusion.place, bf16[512,2048]{1,0:T(8,128)(2,1)} %get-tuple-element.202.first, bf16[2048,1536]{1,0:T(8,128)(2,1)} %qkv.1, ...), custom_call_target="tpu_custom_call" | custom-call | flops 1000000 | bytes 1000000 | tf_op jit(solution)/shard_map/pallas_call | solution.py:377
  105.3 8.6 %shard_map.284 = (bf16[512,1024]{1,0:T(8,128)(2,1)}, bf16[512,256]{1,0:T(8,128)(2,1)}, bf16[16,2,64,1024]{3,2,1,0:T(8,128)(2,1)}) custom-call(s32[1]{0:T(128)} %bitcast.9.side, f32[264,2048]{1,0:T(8,128)} %collective-permute-done.2.near, f32[264,2048]{1,0:T(8,128)} %collective-permute-done.3.other, ...), custom_call_target="tpu_custom_call", output_to_operand_aliasing={{2}: (6, {})} | custom-call | flops 1000000 | bytes 1000000 | tf_op jit(solution)/shard_map/pallas_call | solution.py:256
  113.9 5.0 %shard_map.286 = (bf16[512,256]{1,0:T(8,128)(2,1)}, bf16[512,768]{1,0:T(8,128)(2,1)}) custom-call(s32[2]{0:T(128)} %pad_add_fusion.place, bf16[512,256]{1,0:T(8,128)(2,1)} %get-tuple-element.203.queries, bf16[512,256]{1,0:T(8,128)(2,1)} %get-tuple-element.204.keys, bf16[512,256]{1,0:T(8,128)(2,1)} %get-tuple-element.205.values, ...), custom_call_target="tpu_custom_call" | custom-call | flops 1000000 | bytes 1000000 | tf_op jit(solution)/shard_map/pallas_call | solution.py:431
  118.8 18.3 %shard_map.287 = f32[16,128,2176]{2,1,0:T(8,128)} custom-call(s32[1]{0:T(128)} %bitcast.9.side, bf16[16,2,64,1024]{3,2,1,0:T(8,128)(2,1)} %get-tuple-element.192.refs_0_, bf16[16,2,64,1024]{3,2,1,0:T(8,128)(2,1)} %get-tuple-element.197.refs_1_, bf16[16,2,64,1024]{3,2,1,0:T(8,128)(2,1)} %get-tuple-element.198.refs_2_, ...), custom_call_target="tpu_custom_call" | custom-call | flops 1000000 | bytes 1000000 | tf_op jit(solution)/shard_map/pallas_call | solution.py:605
  137.2 15.7 %shard_map.288 = (f32[256,2048]{1,0:T(8,128)}, f32[256,2048]{1,0:T(8,128)}, f32[8,2048]{1,0:T(8,128)}) custom-call(s32[1]{0:T(128)} %bitcast.8.core.half, bf16[512,1536]{1,0:T(8,128)(2,1)} %get-tuple-element.216.refs_7_.packed, bf16[512,2048]{1,0:T(8,128)(2,1)} %get-tuple-element.217.refs_3_.up_grad, bf16[2048,1536]{1,0:T(8,128)(2,1)} %qkv.1, ...), custom_call_target="tpu_custom_call" | custom-call | flops 1000000 | bytes 1000000 | tf_op jit(solution)/shard_map/pallas_call | solution.py:478
  153.2 4.1 %collective-permute-done.11 = f32[256,2048]{1,0:T(8,128)S(1)} collective-permute-done((f32[256,2048]{1,0:T(8,128)}, f32[256,2048]{1,0:T(8,128)S(1)}, u32[]{:S(2)}, u32[]{:S(2)}) %collective-permute-start.11) | collective-permute-done | bytes 2097184 | tf_op jit(solution)/shard_map/ppermute | solution.py:27
  157.3 3.3 %add.77 = f32[256,2048]{1,0:T(8,128)} add(f32[256,2048]{1,0:T(8,128)} %get-tuple-element.222, f32[256,2048]{1,0:T(8,128)S(1)} %collective-permute-done.11) | non-fusion elementwise | flops 524288 | bytes 6291456 | tf_op jit(solution)/shard_map/add | solution.py:771
  160.5 2.8 %collective-permute-start.12 = (f32[256,2048]{1,0:T(8,128)}, f32[256,2048]{1,0:T(8,128)}, u32[]{:S(2)}, u32[]{:S(2)}) collective-permute-start(f32[256,2048]{1,0:T(8,128)} %add.77), channel_id=1, source_target_pairs={{0,2},{2,0},{1,3},{3,1},{4,6},{6,4},{5,7},{7,5},{8,10},{10,8},{9,1... | collective-permute-start | bytes 6291464 | tf_op jit(solution)/shard_map/ppermute | solution.py:27
  170.4 4.2 %collective-permute-done.4 = f32[32,512]{1,0:T(8,128)S(1)} collective-permute-done((f32[32,512]{1,0:T(8,128)S(1)}, f32[32,512]{1,0:T(8,128)S(1)}, u32[]{:S(2)}, u32[]{:S(2)}) %collective-permute-start.4) | collective-permute-done | bytes 65568 | tf_op jit(solution)/shard_map/ppermute | solution.py:31
  174.6 3.1 %collective-permute-start.5 = (f32[32,512]{1,0:T(8,128)S(1)}, f32[32,512]{1,0:T(8,128)S(1)}, u32[]{:S(2)}, u32[]{:S(2)}) collective-permute-start(f32[32,512]{1,0:T(8,128)S(1)} %add.65), channel_id=1, source_target_pairs={{0,32},{16,48},{32,0},{48,16},{1,33},{17,49},{33,1},{49,17},{2,34}... | collective-permute-start | bytes 196616 | tf_op jit(solution)/shard_map/ppermute | solution.py:31
  177.7 4.5 %collective-permute-done.5 = f32[32,512]{1,0:T(8,128)S(1)} collective-permute-done((f32[32,512]{1,0:T(8,128)S(1)}, f32[32,512]{1,0:T(8,128)S(1)}, u32[]{:S(2)}, u32[]{:S(2)}) %collective-permute-start.5) | collective-permute-done | bytes 65568 | tf_op jit(solution)/shard_map/ppermute | solution.py:31
  187.6 3.6 %collective-permute-start.7 = (f32[32,512]{1,0:T(8,128)S(1)}, f32[32,512]{1,0:T(8,128)S(1)}, u32[]{:S(2)}, u32[]{:S(2)}) collective-permute-start(f32[32,512]{1,0:T(8,128)S(1)} %add.67), channel_id=1, source_target_pairs={{0,8},{4,12},{8,0},{12,4},{1,9},{5,13},{9,1},{13,5},{2,10},{6,14},... | collective-permute-start | bytes 196616 | tf_op jit(solution)/shard_map/ppermute | solution.py:31
  191.2 3.6 %collective-permute-done.7 = f32[32,512]{1,0:T(8,128)S(1)} collective-permute-done((f32[32,512]{1,0:T(8,128)S(1)}, f32[32,512]{1,0:T(8,128)S(1)}, u32[]{:S(2)}, u32[]{:S(2)}) %collective-permute-start.7) | collective-permute-done | bytes 65568 | tf_op jit(solution)/shard_map/ppermute | solution.py:31
  195.8 29.2 %collective-permute-done.8 = f32[1,512]{1,0:T(1,128)S(1)} collective-permute-done((f32[1,512]{1,0:T(1,128)S(1)}, f32[1,512]{1,0:T(1,128)S(1)}, u32[]{:S(2)}, u32[]{:S(2)}) %collective-permute-start.8) | collective-permute-done | bytes 2080 | tf_op jit(solution)/shard_map/ppermute | solution.py:27
  226.3 2.9 %collective-permute-start.10 = (f32[256]{0:T(256)S(1)}, f32[256]{0:T(256)S(1)}, u32[]{:S(2)}, u32[]{:S(2)}) collective-permute-start(f32[256]{0:T(256)S(1)} %add.75), channel_id=1, source_target_pairs={{0,2},{2,0},{1,3},{3,1},{4,6},{6,4},{5,7},{7,5},{8,10},{10,8},{9,1... | collective-permute-start | bytes 3080 | tf_op jit(solution)/shard_map/ppermute | solution.py:27
  232.2 2.6 add.79.combined
  238.6 3.9 %shard_map.289 = (f32[512,2048]{1,0:T(8,128)}, f32[512,2048]{1,0:T(8,128)}) custom-call(s32[1]{0:T(128)} %bitcast.8.core.half, f32[512,2048]{1,0:T(8,128)S(1)} %copy-done, f32[256,2048]{1,0:T(8,128)S(1)} %add.79.combined, bf16[512,2048]{1,0:T(8,128)(2,1)} %hidden.4, bf16[512,2048]{1,0:T(8,128)(2,1)} %cot.3, f32[512,128]{1,0:T(8,128)S(1)} %get-tuple-element.218.stats, ...), custom_call_target="tpu_custom_call" | custom-call | flops 1000000 | bytes 1000000 | tf_op jit(solution)/shard_map/pallas_call | solution.py:536
  244.3 3.8 %shard_map.290 = (f32[512,2048]{1,0:T(8,128)}, f32[512,2048]{1,0:T(8,128)}) custom-call(s32[1]{0:T(128)S(6)} %sub.8.half, f32[512,2048]{1,0:T(8,128)S(1)} %copy-done.1, f32[256,2048]{1,0:T(8,128)} %collective-permute-done.14.combined, bf16[512,2048]{1,0:T(8,128)(2,1)S(1)} %copy-done.7, ...), custom_call_target="tpu_custom_call", output_to_operand_aliasing={{0}: (8, {}), {1}: (9, {})} | custom-call | flops 1000000 | bytes 1000000 | tf_op jit(solution)/shard_map/pallas_call | solution.py:536
  248.1 9.3 %reduce-scatter.9.cloned.1.call-done.near = f32[1,128,2176]{2,1,0:T(8,128)} async-done(((f32[16,128,2176]{2,1,0:T(8,128)}), f32[1,128,2176]{2,1,0:T(8,128)}) %reduce-scatter.9.cloned.1.call-update) | async-done | bytes 1114128 | tf_op jit(solution)/shard_map/optimization_barrier | solution.py:813
  260.8 11.9 %collective-permute-done.15.far = f32[64,2176]{1,0:T(8,128)S(1)} collective-permute-done((f32[64,2176]{1,0:T(8,128)S(1)}, f32[64,2176]{1,0:T(8,128)S(1)}, u32[]{:S(2)}, u32[]{:S(2)}) %collective-permute-start.15) | collective-permute-done | bytes 557088 | tf_op jit(solution)/shard_map/ppermute | solution.py:27
  (129 shorter events, 35.2 us)
Async XLA Ops:
  8.0 129.1 %reduce-scatter.7.cloned.1.call-start = ((), (), s32[]{:S(2)}) async-start(), calls=%async_computation.3 | async-start | bytes 15597568
  25.7 205.7 %all-reduce.5.cloned.1.call-start = ((), (), s32[]{:S(2)}) async-start(), calls=%async_computation.2 | async-start | bytes 8388608 | tf_op jit(solution)/shard_map/psum | solution.py:729
  28.6 48.1 %collective-permute-start = (f32[256,2048]{1,0:T(8,128)}, f32[256,2048]{1,0:T(8,128)}, u32[]{:S(2)}, u32[]{:S(2)}) collective-permute-start(f32[256,2048]{1,0:T(8,128)} %dynamic-slice_convert_fusion.1), channel_id=1, source_target_pairs={{0,64},{64,0},{1,65},{65,1},{2,66},{66,2},{3,67},{67,3},{4,68},{68... | collective-permute-start | bytes 6291464 | tf_op jit(solution)/shard_map/ppermute | solution.py:27
  32.5 50.0 %collective-permute-start.2 = (f32[264,2048]{1,0:T(8,128)}, f32[264,2048]{1,0:T(8,128)}, u32[]{:S(2)}, u32[]{:S(2)}) collective-permute-start(f32[264,2048]{1,0:T(8,128)} %select_maximum_fusion), channel_id=1, source_target_pairs={{0,66},{2,64},{64,2},{66,0},{1,67},{3,65},{65,3},{67,1},{4,70},{6,... | collective-permute-start | bytes 6488072 | tf_op jit(solution)/shard_map/ppermute | solution.py:705
  35.1 9.1 %copy-start.8 = (bf16[512,2048]{1,0:T(8,128)(2,1)S(1)}, bf16[512,2048]{1,0:T(8,128)(2,1)}, u32[]{:S(2)}) copy-start(bf16[512,2048]{1,0:T(8,128)(2,1)} %get-tuple-element.56.hidden) | copy-start | bytes 6291460 | tf_op jit(solution)/shard_map/cond
  49.8 8.5 %copy-start.11 = (bf16[512,2048]{1,0:T(8,128)(2,1)S(1)}, bf16[512,2048]{1,0:T(8,128)(2,1)}, u32[]{:S(2)}) copy-start(bf16[512,2048]{1,0:T(8,128)(2,1)} %get-tuple-element.77.refs_1_.dense) | copy-start | bytes 6291460 | tf_op jit(solution)/shard_map/cond
  58.3 8.8 %copy-start.14 = (bf16[512,2048]{1,0:T(8,128)(2,1)S(1)}, bf16[512,2048]{1,0:T(8,128)(2,1)}, u32[]{:S(2)}) copy-start(bf16[512,2048]{1,0:T(8,128)(2,1)} %get-tuple-element.82.act) | copy-start | bytes 6291460 | tf_op jit(solution)/shard_map/cond
  76.8 5.8 %collective-permute-start.1 = (f32[256,2048]{1,0:T(8,128)}, f32[256,2048]{1,0:T(8,128)}, u32[]{:S(2)}, u32[]{:S(2)}) collective-permute-start(f32[256,2048]{1,0:T(8,128)} %collective-permute-done.near), channel_id=1, source_target_pairs={{0,1},{1,0},{2,3},{3,2},{4,5},{5,4},{6,7},{7,6},{8,9},{9,8},{10,11... | collective-permute-start | bytes 6291464 | tf_op jit(solution)/shard_map/ppermute | solution.py:27
  76.8 180.6 %reduce-scatter.9.cloned.1.call-start = ((), (), s32[]{:S(2)}) async-start(), calls=%async_computation.4 | async-start | bytes 18939904
  82.5 22.7 %collective-permute-start.3 = (f32[264,2048]{1,0:T(8,128)}, f32[264,2048]{1,0:T(8,128)}, u32[]{:S(2)}, u32[]{:S(2)}) collective-permute-start(f32[264,2048]{1,0:T(8,128)} %collective-permute-done.2.near), channel_id=1, source_target_pairs={{0,1},{1,0},{2,3},{3,2},{4,5},{5,4},{6,7},{7,6},{8,9},{9,8},{10,11... | collective-permute-start | bytes 6488072 | tf_op jit(solution)/shard_map/ppermute | solution.py:27
  99.0 6.2 %copy-start.10 = (bf16[512,2048]{1,0:T(8,128)(2,1)S(1)}, bf16[512,2048]{1,0:T(8,128)(2,1)}, u32[]{:S(2)}) copy-start(bf16[512,2048]{1,0:T(8,128)(2,1)} %dense.1) | copy-start | bytes 6291460
  105.3 13.6 %copy-start.13 = (bf16[512,2048]{1,0:T(8,128)(2,1)S(1)}, bf16[512,2048]{1,0:T(8,128)(2,1)}, u32[]{:S(2)}) copy-start(bf16[512,2048]{1,0:T(8,128)(2,1)} %get-tuple-element.186.refs_9_) | copy-start | bytes 6291460
  152.9 4.4 %collective-permute-start.11 = (f32[256,2048]{1,0:T(8,128)}, f32[256,2048]{1,0:T(8,128)S(1)}, u32[]{:S(2)}, u32[]{:S(2)}) collective-permute-start(f32[256,2048]{1,0:T(8,128)} %get-tuple-element.223), channel_id=1, source_target_pairs={{0,1},{1,0},{2,3},{3,2},{4,5},{5,4},{6,7},{7,6},{8,9},{9,8},{10,11... | collective-permute-start | bytes 6291464 | tf_op jit(solution)/shard_map/ppermute | solution.py:27
  160.5 71.6 %collective-permute-start.12 = (f32[256,2048]{1,0:T(8,128)}, f32[256,2048]{1,0:T(8,128)}, u32[]{:S(2)}, u32[]{:S(2)}) collective-permute-start(f32[256,2048]{1,0:T(8,128)} %add.77), channel_id=1, source_target_pairs={{0,2},{2,0},{1,3},{3,1},{4,6},{6,4},{5,7},{7,5},{8,10},{10,8},{9,1... | collective-permute-start | bytes 6291464 | tf_op jit(solution)/shard_map/ppermute | solution.py:27
  165.7 18.5 %copy-start.17 = (f32[1,128,1792]{2,1,0:T(8,128)S(1)}, f32[1,128,1792]{2,1,0:T(8,128)}, u32[]{:S(2)}) copy-start(f32[1,128,1792]{2,1,0:T(8,128)} %reduce-scatter.7.cloned.1.call-done) | copy-start | bytes 2752516
  168.8 5.7 %collective-permute-start.4 = (f32[32,512]{1,0:T(8,128)S(1)}, f32[32,512]{1,0:T(8,128)S(1)}, u32[]{:S(2)}, u32[]{:S(2)}) collective-permute-start(f32[32,512]{1,0:T(8,128)S(1)} %concatenate.27), channel_id=1, source_target_pairs={{0,16},{16,0},{32,48},{48,32},{1,17},{17,1},{33,49},{49,33},{2,18}... | collective-permute-start | bytes 196616 | tf_op jit(solution)/shard_map/ppermute | solution.py:31
  174.6 7.6 %collective-permute-start.5 = (f32[32,512]{1,0:T(8,128)S(1)}, f32[32,512]{1,0:T(8,128)S(1)}, u32[]{:S(2)}, u32[]{:S(2)}) collective-permute-start(f32[32,512]{1,0:T(8,128)S(1)} %add.65), channel_id=1, source_target_pairs={{0,32},{16,48},{32,0},{48,16},{1,33},{17,49},{33,1},{49,17},{2,34}... | collective-permute-start | bytes 196616 | tf_op jit(solution)/shard_map/ppermute | solution.py:31
  182.2 5.4 %collective-permute-start.6 = (f32[32,512]{1,0:T(8,128)S(1)}, f32[32,512]{1,0:T(8,128)S(1)}, u32[]{:S(2)}, u32[]{:S(2)}) collective-permute-start(f32[32,512]{1,0:T(8,128)S(1)} %add.66), channel_id=1, source_target_pairs={{0,4},{4,0},{8,12},{12,8},{1,5},{5,1},{9,13},{13,9},{2,6},{6,2},{1... | collective-permute-start | bytes 196616 | tf_op jit(solution)/shard_map/ppermute | solution.py:31
  184.3 47.1 %collective-permute-start.13 = (f32[64,1792]{1,0:T(8,128)S(1)}, f32[64,1792]{1,0:T(8,128)S(1)}, u32[]{:S(2)}, u32[]{:S(2)}) collective-permute-start(f32[64,1792]{1,0:T(8,128)S(1)} %dynamic-slice_bitcast_fusion.1), channel_id=1, source_target_pairs={{0,64},{64,0},{1,65},{65,1},{2,66},{66,2},{3,67},{67,3},{4,68},{68... | collective-permute-start | bytes 1376264 | tf_op jit(solution)/shard_map/ppermute | solution.py:27
  187.6 7.3 %collective-permute-start.7 = (f32[32,512]{1,0:T(8,128)S(1)}, f32[32,512]{1,0:T(8,128)S(1)}, u32[]{:S(2)}, u32[]{:S(2)}) collective-permute-start(f32[32,512]{1,0:T(8,128)S(1)} %add.67), channel_id=1, source_target_pairs={{0,8},{4,12},{8,0},{12,4},{1,9},{5,13},{9,1},{13,5},{2,10},{6,14},... | collective-permute-start | bytes 196616 | tf_op jit(solution)/shard_map/ppermute | solution.py:31
  194.9 30.1 %collective-permute-start.8 = (f32[1,512]{1,0:T(1,128)S(1)}, f32[1,512]{1,0:T(1,128)S(1)}, u32[]{:S(2)}, u32[]{:S(2)}) collective-permute-start(f32[1,512]{1,0:T(1,128)S(1)} %constant_dynamic-slice_fusion), channel_id=1, source_target_pairs={{0,64},{64,0},{1,65},{65,1},{2,66},{66,2},{3,67},{67,3},{4,68},{68... | collective-permute-start | bytes 6152 | tf_op jit(solution)/shard_map/ppermute | solution.py:27
  225.0 1.2 collective-permute-start.9
  226.3 5.1 %collective-permute-start.10 = (f32[256]{0:T(256)S(1)}, f32[256]{0:T(256)S(1)}, u32[]{:S(2)}, u32[]{:S(2)}) collective-permute-start(f32[256]{0:T(256)S(1)} %add.75), channel_id=1, source_target_pairs={{0,2},{2,0},{1,3},{3,1},{4,6},{6,4},{5,7},{7,5},{8,10},{10,8},{9,1... | collective-permute-start | bytes 3080 | tf_op jit(solution)/shard_map/ppermute | solution.py:27
  231.3 5.0 %copy-start.3 = (f32[2048]{0:T(1024)S(1)}, f32[2048]{0:T(1024)}, u32[]{:S(2)}) copy-start(f32[2048]{0:T(1024)} %param.28) | copy-start | bytes 24580
  231.3 5.0 %copy-start.4 = (f32[2048]{0:T(1024)S(1)}, f32[2048]{0:T(1024)}, u32[]{:S(2)}) copy-start(f32[2048]{0:T(1024)} %param.34) | copy-start | bytes 24580
  234.7 7.8 %collective-permute-start.14 = (f32[256,2048]{1,0:T(8,128)S(1)}, f32[256,2048]{1,0:T(8,128)}, u32[]{:S(2)}, u32[]{:S(2)}) collective-permute-start(f32[256,2048]{1,0:T(8,128)S(1)} %add.79.combined), channel_id=1, source_target_pairs={{0,1},{1,0},{2,3},{3,2},{4,5},{5,4},{6,7},{7,6},{8,9},{9,8},{10,11... | collective-permute-start | bytes 6291464 | tf_op jit(solution)/shard_map/ppermute | solution.py:27
  235.6 38.3 %copy-start.29 = (f32[64]{0:T(128)}, f32[64]{0:T(128)S(1)}, u32[]{:S(2)}) copy-start(f32[64]{0:T(128)S(1)} %get-tuple-element.333) | copy-start | bytes 772
  238.6 5.0 %copy-start.6 = (bf16[512,2048]{1,0:T(8,128)(2,1)S(1)}, bf16[512,2048]{1,0:T(8,128)(2,1)}, u32[]{:S(2)}) copy-start(bf16[512,2048]{1,0:T(8,128)(2,1)} %cot.3) | copy-start | bytes 6291460
  238.6 5.7 %copy-start.7 = (bf16[512,2048]{1,0:T(8,128)(2,1)S(1)}, bf16[512,2048]{1,0:T(8,128)(2,1)}, u32[]{:S(2)}) copy-start(bf16[512,2048]{1,0:T(8,128)(2,1)} %hidden.4) | copy-start | bytes 6291460
  244.3 16.5 %copy-start.19 = (f32[64,1792]{1,0:T(8,128)S(1)}, f32[64,1792]{1,0:T(8,128)}, u32[]{:S(2)}) copy-start(f32[64,1792]{1,0:T(8,128)} %copy-done.18) | copy-start | bytes 1376260
  257.4 15.3 %copy-start.2 = (f32[1,128,2176]{2,1,0:T(8,128)S(1)}, f32[1,128,2176]{2,1,0:T(8,128)}, u32[]{:S(2)}) copy-start(f32[1,128,2176]{2,1,0:T(8,128)} %reduce-scatter.9.cloned.1.call-done.near) | copy-start | bytes 3342340
  258.6 14.1 %collective-permute-start.15 = (f32[64,2176]{1,0:T(8,128)S(1)}, f32[64,2176]{1,0:T(8,128)S(1)}, u32[]{:S(2)}, u32[]{:S(2)}) collective-permute-start(f32[64,2176]{1,0:T(8,128)S(1)} %dynamic-slice_bitcast_fusion), channel_id=1, source_target_pairs={{0,64},{64,0},{1,65},{65,1},{2,66},{66,2},{3,67},{67,3},{4,68},{68... | collective-permute-start | bytes 1671176 | tf_op jit(solution)/shard_map/ppermute | solution.py:27
  (14 other events, 54.5 us)
Sparse Core Ops, SparseCore 0:
  25.8 104.0 reduce-scatter.6
  137.3 120.0 reduce-scatter.8
Sparse Core Ops, SparseCore 1:
  76.9 100.6 all-reduce.4
where the time goes:
time: 283 us; the launch traced here: 282 us
  Pallas kernels  136 us (48%)
  waiting for transfers between devices  78.2 us (28%)
  starting transfers between devices  24.6 us (9%)
  between operations  15.9 us (6%)
  other arithmetic  15.5 us (5%)
  local copies, waits for them, and re-layouts  11.8 us (4%)
    ppermute x11, waiting for transfers between devices, send(): return lax.ppermute(value, axis, [(i, (i + step) % n) for i in range(n)])  48.5 us
    pallas_call x1, Pallas kernels, joint(): pl.pallas_call(joint_kernel, grid_spec=pltpu.PrefetchScalarGridSpec(num_s...  18.3 us
    pallas_call x1, Pallas kernels, feed(): pl.pallas_call(feed_kernel, grid=(units // width,), in_specs=[whole((TOK,...  17.6 us
    pallas_call x1, Pallas kernels, halves_call(): pl.pallas_call(kernel, grid_spec=pltpu.PrefetchScalarGridSpec(num_scalar_...  15.7 us
    pallas_call x2, Pallas kernels, project(): pl.pallas_call(project_kernel, grid_spec=pltpu.PrefetchScalarGridSpec(num...  14.7 us
    ppermute x4, waiting for transfers between devices, swap(): return lax.ppermute(value, axis, [(i, i ^ bit) for i in range(SIZES[axis])])  14.6 us
    pallas_call x2, Pallas kernels, attend(): pl.pallas_call(attend_kernel, grid_spec=pltpu.PrefetchScalarGridSpec(num_...  13.8 us
    ppermute x11, starting transfers between devices, send(): return lax.ppermute(value, axis, [(i, (i + step) % n) for i in range(n)])  11.7 us
  transfers between devices with their start and end apart: 19, of which 11 were waited for; matrix products, arithmetic and copies ran while one was open for 7% of the time, Pallas kernels for 42%

commit v1 on v0

--- a/solution.py
+++ b/solution.py
@@ -63,6 +63,37 @@
     centred = hidden - average
     inv_std = lax.rsqrt(jnp.mean(centred * centred, axis=-1, keepdims=True) + EPSILON)
     return centred * inv_std, average, inv_std
+
+
+def sent_kernel(core, hidden, cot, marks, hidden_out, cot_out):
+    half = TOK // 2
+    hidden_out[...] = hidden[...].astype(F32)
+    cot_out[:half] = cot[...].astype(F32)
+    row = jnp.concatenate([marks[...], jnp.zeros((1, D - 2 * TOK), F32)], axis=1)
+    cot_out[half : half + 8] = jnp.broadcast_to(row, (8, D))
+
+
+def sent(core, hidden, cot, marks):
+    half = TOK // 2
+    rows = pl.BlockSpec((half, D), lambda i, s: (s[0], 0))
+    return pl.pallas_call(
+        sent_kernel,
+        grid_spec=pltpu.PrefetchScalarGridSpec(
+            num_scalar_prefetch=1,
+            grid=(1,),
+            in_specs=[rows, rows, pl.BlockSpec((1, 2 * TOK), lambda i, s: (0, 0))],
+            out_specs=[
+                pl.BlockSpec((half, D), lambda i, s: (0, 0)),
+                pl.BlockSpec((half + 8, D), lambda i, s: (0, 0)),
+            ],
+        ),
+        out_shape=[
+            jax.ShapeDtypeStruct((half, D), F32),
+            jax.ShapeDtypeStruct((half + 8, D), F32),
+        ],
+        compiler_params=pltpu.CompilerParams(vmem_limit_bytes=VMEM),
+        cost_estimate=COST,
+    )(core, hidden, cot, marks)
 
 
 def first_kernel(
@@ -697,11 +728,9 @@
     down_sum = after(lax.psum_scatter(down_grad, ("x", "y"), scatter_dimension=0, tiled=True))
     _, cotangent, hidden_in = after((down_grad, cotangent, hidden_in))
 
-    hidden_got = send(of_core(hidden_in, core).astype(F32), "zl")
     marks = jnp.concatenate([segment_ids, positions]).astype(F32).reshape(1, 2 * TOK)
-    cot_sent = jnp.concatenate(
-        [of_core(cotangent, core).astype(F32), jnp.pad(marks, ((0, 7), (0, D - 2 * TOK)))], axis=0
-    )
+    hidden_sent, cot_sent = sent(at_core, hidden_in, cotangent, marks)
+    hidden_got = send(hidden_sent, "zl")
     cot_got = lax.ppermute(cot_sent, ("zl", "zh"), [(i, 3 - i) for i in range(4)])
 
     own_marks = marks.reshape(2, TOK)

time: 283 us -> 284 us (level)
  other arithmetic: 15.5 us -> 11.4 us
  Pallas kernels: 136 us -> 139 us
    pallas_call x0 -> x1, Pallas kernels: none -> 3.41 us  [sent(): pl.pallas_call(sent_kernel, grid_spec=pltpu.PrefetchScalarGridSpec(num_sc...]
    convert_element_type x2 -> x0, other arithmetic: 3.16 us -> none  [the longest x1 2.91 us: body(): hidden_got = send(of_core(hidden_in, core).astype(F32), 'zl')]
  transfers between devices with their start and end apart: 19 -> 19, of which waited for: 11 -> 13; matrix products, arithmetic and copies ran while one was open for 7% -> 6% of each run, Pallas kernels for 42% -> 42%
where the time goes in v1:
time: 284 us
  Pallas kernels  139 us (49%)
  waiting for transfers between devices  78.4 us (28%)
  starting transfers between devices  26.4 us (9%)
  between operations  15.8 us (6%)
  local copies, waits for them, and re-layouts  12.7 us (4%)
  other arithmetic  11.4 us (4%)
    ppermute x11, waiting for transfers between devices, send(): return lax.ppermute(value, axis, [(i, (i + step) % n) for i in range(n)])  51 us
    pallas_call x1, Pallas kernels, joint(): pl.pallas_call(joint_kernel, grid_spec=pltpu.PrefetchScalarGridSpec(num_s...  18.3 us
    pallas_call x1, Pallas kernels, feed(): pl.pallas_call(feed_kernel, grid=(units // width,), in_specs=[whole((TOK,...  17.6 us
    pallas_call x1, Pallas kernels, halves_call(): pl.pallas_call(kernel, grid_spec=pltpu.PrefetchScalarGridSpec(num_scalar_...  15.3 us
    pallas_call x2, Pallas kernels, project(): pl.pallas_call(project_kernel, grid_spec=pltpu.PrefetchScalarGridSpec(num...  14.6 us
    ppermute x4, waiting for transfers between devices, swap(): return lax.ppermute(value, axis, [(i, i ^ bit) for i in range(SIZES[axis])])  14.5 us
    pallas_call x2, Pallas kernels, attend(): pl.pallas_call(attend_kernel, grid_spec=pltpu.PrefetchScalarGridSpec(num_...  13.8 us
    ppermute x11, starting transfers between devices, send(): return lax.ppermute(value, axis, [(i, (i + step) % n) for i in range(n)])  13 us
  transfers between devices with their start and end apart: 19, of which 13 were waited for; matrix products, arithmetic and copies ran while one was open for 6% of the time, Pallas kernels for 42%

profile of v1, /device:TPU:0, one launch (start us, length us, event | category | flops | bytes accessed | tf_op | source)
XLA Modules:
  0.0 283.6 jit_solution(18252785169127020013)
XLA Ops:
  8.1 17.6 %shard_map.281 = (bf16[512,2048]{1,0:T(8,128)(2,1)}, f32[512,2048]{1,0:T(8,128)}, f32[16,128,1792]{2,1,0:T(8,128)}) custom-call(bf16[512,2048]{1,0:T(8,128)(2,1)} %hidden.5, f32[1,2048]{1,0:T(1,128)} %bitcast.47, f32[1,2048]{1,0:T(1,128)} %bitcast.58, bf16[512,2048]{1,0:T(8,128)(2,1)} %cot.4, bf16[2048,2048]{1,0:T(8,128)(2,1)} %up.1, f32[2,8,128]{2,1,0:T(8,128)} %bitcast.68), custom_call_target="tpu_custom_call" | custom-call | flops 1000000 | bytes 1000000 | tf_op jit(solution)/shard_map/pallas_call | solution.py:222
  27.3 3.4 %shard_map.282 = (f32[256,2048]{1,0:T(8,128)}, f32[264,2048]{1,0:T(8,128)}) custom-call(s32[1]{0:T(128)} %bitcast.8.core.half, bf16[512,2048]{1,0:T(8,128)(2,1)} %hidden.5, bf16[512,2048]{1,0:T(8,128)(2,1)S(1)} %copy-done.5, f32[1,1024]{1,0:T(1,128)} %add_convert_fusion.marks), custom_call_target="tpu_custom_call" | custom-call | flops 1000000 | bytes 1000000 | tf_op jit(solution)/shard_map/pallas_call | solution.py:79
  32.7 2.5 collective-permute-start.2
  35.3 41.8 %conditional.1 = (bf16[16,2,64,1024]{3,2,1,0:T(8,128)(2,1)}, bf16[16,2,64,1024]{3,2,1,0:T(8,128)(2,1)}, bf16[16,2,64,1024]{3,2,1,0:T(8,128)(2,1)}, f32[512,128]{...) conditional(s32[]{:T(128)} %convert_element_type.29, ...), branch_computations={%region_0.0_spmd, %region_1.0_spmd} | conditional | flops 5000000 | bytes 30165984 | solution.py:757
  35.3 9.2 %branch_0_fun.8 = bf16[512,2048]{1,0:T(8,128)(2,1)} custom-call(bf16[512,2048]{1,0:T(8,128)(2,1)S(1)} %get-tuple-element.57.cot.refs_0_, bf16[2048,2048]{1,0:T(8,128)(2,1)} %get-tuple-element.80.weight.down, f32[512,2048]{1,0:T(8,128)} %get-tuple-element.81.slope), custom_call_target="tpu_custom_call" | custom-call | flops 1000000 | bytes 1000000 | tf_op jit(solution)/shard_map/cond/branch_0_fun/pallas_call | solution.py:259
  44.5 5.0 %branch_0_fun.5 = (bf16[512,2048]{1,0:T(8,128)(2,1)}, bf16[16,2,64,1024]{3,2,1,0:T(8,128)(2,1)}, bf16[16,2,64,1024]{3,2,1,0:T(8,128)(2,1)}, bf16[16,2,64,1024]{3,2,1,0:T(8,128)(2,1)}, f32[512,128]{1,0:T(8,128)S(1)}) custom-call(bf16[512,2048]{1,0:T(8,128)(2,1)S(1)} %copy-done.8, bf16[512,2048]{1,0:T(8,128)(2,1)S(1)} %get-tuple-element.57.cot.refs_0_, ...), custom_call_target="tpu_custom_call" | custom-call | flops 1000000 | bytes 1000000 | tf_op jit(solution)/shard_map/cond/branch_0_fun/pallas_call | solution.py:149
  50.0 8.5 %branch_0_fun.6 = (bf16[512,512]{1,0:T(8,128)(2,1)}, bf16[512,512]{1,0:T(8,128)(2,1)}, bf16[512,512]{1,0:T(8,128)(2,1)}, f32[512,128]{1,0:T(8,128)}, f32[512,128]{1,0:T(8,128)}, /*index=5*/f32[512,128]{1,0:T(8,128)}) custom-call(s32[2]{0:T(128)} %broadcast_1_place.0.place, bf16[512,2048]{1,0:T(8,128)(2,1)} %get-tuple-element.66.first, ...), custom_call_target="tpu_custom_call" | custom-call | flops 1000000 | bytes 1000000 | tf_op jit(solution)/shard_map/cond/branch_0_fun/pallas_call | solution.py:408
  58.5 8.8 %branch_0_fun.7 = (bf16[512,512]{1,0:T(8,128)(2,1)}, bf16[512,1536]{1,0:T(8,128)(2,1)}) custom-call(s32[2]{0:T(128)} %broadcast_1_place.0.place, bf16[512,512]{1,0:T(8,128)(2,1)} %get-tuple-element.71.queries, bf16[512,512]{1,0:T(8,128)(2,1)} %get-tuple-element.72.keys, bf16[512,512]{1,0:T(8,128)(2,1)} %get-tuple-element.73.values, ...), custom_call_target="tpu_custom_call" | custom-call | flops 1000000 | bytes 1000000 | tf_op jit(solution)/shard_map/cond/branch_0_fun/pallas_call | solution.py:462
  67.4 9.7 %branch_0_fun.9 = f32[512,2048]{1,0:T(8,128)} custom-call(bf16[512,512]{1,0:T(8,128)(2,1)} %get-tuple-element.298.mixed, bf16[512,2048]{1,0:T(8,128)(2,1)S(1)} %copy-done.14, bf16[512,2048]{1,0:T(8,128)(2,1)S(1)} %copy-done.11, bf16[2048,2048]{1,0:T(8,128)(2,1)} %get-tuple-element.80.weight.down), custom_call_target="tpu_custom_call" | custom-call | flops 1000000 | bytes 1000000 | tf_op jit(solution)/shard_map/cond/branch_0_fun/pallas_call | solution.py:527
  78.7 4.0 %collective-permute-done.2.near = f32[264,2048]{1,0:T(8,128)} collective-permute-done((f32[264,2048]{1,0:T(8,128)}, f32[264,2048]{1,0:T(8,128)}, u32[]{:S(2)}, u32[]{:S(2)}) %collective-permute-start.2) | collective-permute-done | bytes 2162720 | tf_op jit(solution)/shard_map/ppermute | solution.py:734
  85.4 7.8 %shard_map.283 = (bf16[512,2048]{1,0:T(8,128)(2,1)}, bf16[512,2048]{1,0:T(8,128)(2,1)}, bf16[16,2,64,1024]{3,2,1,0:T(8,128)(2,1)}, bf16[16,2,64,1024]{3,2,1,0:T(8,128)(2,1)}) custom-call(f32[256,2048]{1,0:T(8,128)} %collective-permute-done.near, f32[256,2048]{1,0:T(8,128)} %collective-permute-done.1.other, ...), custom_call_target="tpu_custom_call", output_to_operand_aliasing={{2}: (6, {}), {3}: (7, {})} | custom-call | flops 1000000 | bytes 1000000 | tf_op jit(solution)/shard_map/pallas_call | solution.py:167
  93.2 6.5 %shard_map.284 = (f32[512,1024]{1,0:T(8,128)}, bf16[512,128]{1,0:T(8,128)(2,1)}) custom-call(s32[1]{0:T(128)} %bitcast.9.side, bf16[512,2048]{1,0:T(8,128)(2,1)} %get-tuple-element.198.second, bf16[2048,2048]{1,0:T(8,128)(2,1)} %up.1, f32[4,4,128]{2,1,0:T(4,128)} %bitcast.69), custom_call_target="tpu_custom_call" | custom-call | flops 1000000 | bytes 1000000 | tf_op jit(solution)/shard_map/pallas_call | solution.py:332
  99.7 6.1 %shard_map.286 = (bf16[512,256]{1,0:T(8,128)(2,1)}, bf16[512,256]{1,0:T(8,128)(2,1)}, bf16[512,256]{1,0:T(8,128)(2,1)}, f32[512,128]{1,0:T(8,128)}, f32[512,128]{1,0:T(8,128)}, /*index=5*/f32[512,128]{1,0:T(8,128)}) custom-call(s32[2]{0:T(128)} %pad_add_fusion.place, bf16[512,2048]{1,0:T(8,128)(2,1)} %get-tuple-element.206.first, bf16[2048,1536]{1,0:T(8,128)(2,1)} %qkv.1, ...), custom_call_target="tpu_custom_call" | custom-call | flops 1000000 | bytes 1000000 | tf_op jit(solution)/shard_map/pallas_call | solution.py:408
  105.8 8.5 %shard_map.285 = (bf16[512,1024]{1,0:T(8,128)(2,1)}, bf16[512,256]{1,0:T(8,128)(2,1)}, bf16[16,2,64,1024]{3,2,1,0:T(8,128)(2,1)}) custom-call(s32[1]{0:T(128)} %bitcast.9.side, f32[264,2048]{1,0:T(8,128)} %collective-permute-done.2.near, f32[264,2048]{1,0:T(8,128)} %collective-permute-done.3.other, ...), custom_call_target="tpu_custom_call", output_to_operand_aliasing={{2}: (6, {})} | custom-call | flops 1000000 | bytes 1000000 | tf_op jit(solution)/shard_map/pallas_call | solution.py:287
  114.4 5.0 %shard_map.287 = (bf16[512,256]{1,0:T(8,128)(2,1)}, bf16[512,768]{1,0:T(8,128)(2,1)}) custom-call(s32[2]{0:T(128)} %pad_add_fusion.place, bf16[512,256]{1,0:T(8,128)(2,1)} %get-tuple-element.207.queries, bf16[512,256]{1,0:T(8,128)(2,1)} %get-tuple-element.208.keys, bf16[512,256]{1,0:T(8,128)(2,1)} %get-tuple-element.209.values, ...), custom_call_target="tpu_custom_call" | custom-call | flops 1000000 | bytes 1000000 | tf_op jit(solution)/shard_map/pallas_call | solution.py:462
  119.4 18.3 %shard_map.288 = f32[16,128,2176]{2,1,0:T(8,128)} custom-call(s32[1]{0:T(128)} %bitcast.9.side, bf16[16,2,64,1024]{3,2,1,0:T(8,128)(2,1)} %get-tuple-element.196.refs_0_, bf16[16,2,64,1024]{3,2,1,0:T(8,128)(2,1)} %get-tuple-element.201.refs_1_, bf16[16,2,64,1024]{3,2,1,0:T(8,128)(2,1)} %get-tuple-element.202.refs_2_, ...), custom_call_target="tpu_custom_call" | custom-call | flops 1000000 | bytes 1000000 | tf_op jit(solution)/shard_map/pallas_call | solution.py:636
  137.7 15.3 %shard_map.289 = (f32[256,2048]{1,0:T(8,128)}, f32[256,2048]{1,0:T(8,128)}, f32[8,2048]{1,0:T(8,128)}) custom-call(s32[1]{0:T(128)} %bitcast.8.core.half, bf16[512,1536]{1,0:T(8,128)(2,1)} %get-tuple-element.220.refs_7_.packed, bf16[512,2048]{1,0:T(8,128)(2,1)} %get-tuple-element.221.refs_3_.up_grad, bf16[2048,1536]{1,0:T(8,128)(2,1)} %qkv.1, ...), custom_call_target="tpu_custom_call" | custom-call | flops 1000000 | bytes 1000000 | tf_op jit(solution)/shard_map/pallas_call | solution.py:509
  153.5 4.0 %collective-permute-done.11 = f32[256,2048]{1,0:T(8,128)S(1)} collective-permute-done((f32[256,2048]{1,0:T(8,128)}, f32[256,2048]{1,0:T(8,128)S(1)}, u32[]{:S(2)}, u32[]{:S(2)}) %collective-permute-start.11) | collective-permute-done | bytes 2097184 | tf_op jit(solution)/shard_map/ppermute | solution.py:27
  157.5 3.3 %add.70 = f32[256,2048]{1,0:T(8,128)} add(f32[256,2048]{1,0:T(8,128)} %get-tuple-element.226, f32[256,2048]{1,0:T(8,128)S(1)} %collective-permute-done.11) | non-fusion elementwise | flops 524288 | bytes 6291456 | tf_op jit(solution)/shard_map/add | solution.py:800
  160.8 4.2 %collective-permute-start.12 = (f32[256,2048]{1,0:T(8,128)}, f32[256,2048]{1,0:T(8,128)}, u32[]{:S(2)}, u32[]{:S(2)}) collective-permute-start(f32[256,2048]{1,0:T(8,128)} %add.70), channel_id=1, source_target_pairs={{0,2},{2,0},{1,3},{3,1},{4,6},{6,4},{5,7},{7,5},{8,10},{10,8},{9,1... | collective-permute-start | bytes 6291464 | tf_op jit(solution)/shard_map/ppermute | solution.py:27
  171.9 4.3 %collective-permute-done.4 = f32[32,512]{1,0:T(8,128)S(1)} collective-permute-done((f32[32,512]{1,0:T(8,128)S(1)}, f32[32,512]{1,0:T(8,128)S(1)}, u32[]{:S(2)}, u32[]{:S(2)}) %collective-permute-start.4) | collective-permute-done | bytes 65568 | tf_op jit(solution)/shard_map/ppermute | solution.py:31
  176.2 3.1 %collective-permute-start.5 = (f32[32,512]{1,0:T(8,128)S(1)}, f32[32,512]{1,0:T(8,128)S(1)}, u32[]{:S(2)}, u32[]{:S(2)}) collective-permute-start(f32[32,512]{1,0:T(8,128)S(1)} %add.58), channel_id=1, source_target_pairs={{0,32},{16,48},{32,0},{48,16},{1,33},{17,49},{33,1},{49,17},{2,34}... | collective-permute-start | bytes 196616 | tf_op jit(solution)/shard_map/ppermute | solution.py:31
  179.3 4.5 %collective-permute-done.5 = f32[32,512]{1,0:T(8,128)S(1)} collective-permute-done((f32[32,512]{1,0:T(8,128)S(1)}, f32[32,512]{1,0:T(8,128)S(1)}, u32[]{:S(2)}, u32[]{:S(2)}) %collective-permute-start.5) | collective-permute-done | bytes 65568 | tf_op jit(solution)/shard_map/ppermute | solution.py:31
  188.9 4.3 %collective-permute-start.7 = (f32[32,512]{1,0:T(8,128)S(1)}, f32[32,512]{1,0:T(8,128)S(1)}, u32[]{:S(2)}, u32[]{:S(2)}) collective-permute-start(f32[32,512]{1,0:T(8,128)S(1)} %add.60), channel_id=1, source_target_pairs={{0,8},{4,12},{8,0},{12,4},{1,9},{5,13},{9,1},{13,5},{2,10},{6,14},... | collective-permute-start | bytes 196616 | tf_op jit(solution)/shard_map/ppermute | solution.py:31
  193.2 3.6 %collective-permute-done.7 = f32[32,512]{1,0:T(8,128)S(1)} collective-permute-done((f32[32,512]{1,0:T(8,128)S(1)}, f32[32,512]{1,0:T(8,128)S(1)}, u32[]{:S(2)}, u32[]{:S(2)}) %collective-permute-start.7) | collective-permute-done | bytes 65568 | tf_op jit(solution)/shard_map/ppermute | solution.py:31
  197.4 29.7 %collective-permute-done.8 = f32[1,512]{1,0:T(1,128)S(1)} collective-permute-done((f32[1,512]{1,0:T(1,128)S(1)}, f32[1,512]{1,0:T(1,128)S(1)}, u32[]{:S(2)}, u32[]{:S(2)}) %collective-permute-start.8) | collective-permute-done | bytes 2080 | tf_op jit(solution)/shard_map/ppermute | solution.py:27
  228.3 2.9 %collective-permute-start.10 = (f32[256]{0:T(256)S(1)}, f32[256]{0:T(256)S(1)}, u32[]{:S(2)}, u32[]{:S(2)}) collective-permute-start(f32[256]{0:T(256)S(1)} %add.68), channel_id=1, source_target_pairs={{0,2},{2,0},{1,3},{3,1},{4,6},{6,4},{5,7},{7,5},{8,10},{10,8},{9,1... | collective-permute-start | bytes 3080 | tf_op jit(solution)/shard_map/ppermute | solution.py:27
  234.2 2.6 add.72.combined
  240.6 3.9 %shard_map.290 = (f32[512,2048]{1,0:T(8,128)}, f32[512,2048]{1,0:T(8,128)}) custom-call(s32[1]{0:T(128)} %bitcast.8.core.half, f32[512,2048]{1,0:T(8,128)S(1)} %copy-done, f32[256,2048]{1,0:T(8,128)S(1)} %add.72.combined, bf16[512,2048]{1,0:T(8,128)(2,1)} %hidden.5, bf16[512,2048]{1,0:T(8,128)(2,1)} %cot.4, f32[512,128]{1,0:T(8,128)S(1)} %get-tuple-element.222.stats, ...), custom_call_target="tpu_custom_call" | custom-call | flops 1000000 | bytes 1000000 | tf_op jit(solution)/shard_map/pallas_call | solution.py:567
  246.3 3.8 %shard_map.291 = (f32[512,2048]{1,0:T(8,128)}, f32[512,2048]{1,0:T(8,128)}) custom-call(s32[1]{0:T(128)S(6)} %sub.8.half, f32[512,2048]{1,0:T(8,128)S(1)} %copy-done.1, f32[256,2048]{1,0:T(8,128)} %collective-permute-done.14.combined, bf16[512,2048]{1,0:T(8,128)(2,1)S(1)} %copy-done.7, ...), custom_call_target="tpu_custom_call", output_to_operand_aliasing={{0}: (8, {}), {1}: (9, {})} | custom-call | flops 1000000 | bytes 1000000 | tf_op jit(solution)/shard_map/pallas_call | solution.py:567
  250.2 8.9 %reduce-scatter.9.cloned.1.call-done.near = f32[1,128,2176]{2,1,0:T(8,128)} async-done(((f32[16,128,2176]{2,1,0:T(8,128)}), f32[1,128,2176]{2,1,0:T(8,128)}) %reduce-scatter.9.cloned.1.call-update) | async-done | bytes 1114128 | tf_op jit(solution)/shard_map/optimization_barrier | solution.py:842
  262.5 11.9 %collective-permute-done.15.far = f32[64,2176]{1,0:T(8,128)S(1)} collective-permute-done((f32[64,2176]{1,0:T(8,128)S(1)}, f32[64,2176]{1,0:T(8,128)S(1)}, u32[]{:S(2)}, u32[]{:S(2)}) %collective-permute-start.15) | collective-permute-done | bytes 557088 | tf_op jit(solution)/shard_map/ppermute | solution.py:27
  (127 shorter events, 36.4 us)
Async XLA Ops:
  8.0 129.7 %reduce-scatter.7.cloned.1.call-start = ((), (), s32[]{:S(2)}) async-start(), calls=%async_computation.3 | async-start | bytes 15597568
  25.7 9.5 %copy-start.20 = (f32[2048]{0:T(1024)S(1)}, f32[2048]{0:T(1024)}, u32[]{:S(2)}) copy-start(f32[2048]{0:T(1024)} %param.29) | copy-start | bytes 24580
  25.7 9.5 %copy-start.21 = (f32[32,1]{1,0:T(8,128)S(1)}, f32[32,1]{1,0:T(8,128)}, u32[]{:S(2)}) copy-start(f32[32,1]{1,0:T(8,128)} %constant.47.clone.inverse) | copy-start | bytes 388
  25.7 9.5 %copy-start.22 = (f32[2048]{0:T(1024)S(1)}, f32[2048]{0:T(1024)}, u32[]{:S(2)}) copy-start(f32[2048]{0:T(1024)} %param.23) | copy-start | bytes 24580
  25.7 9.5 %copy-start.23 = (f32[2048]{0:T(1024)S(1)}, f32[2048]{0:T(1024)}, u32[]{:S(2)}) copy-start(f32[2048]{0:T(1024)} %param.30) | copy-start | bytes 24580
  25.7 9.5 %copy-start.24 = (f32[2048]{0:T(1024)S(1)}, f32[2048]{0:T(1024)}, u32[]{:S(2)}) copy-start(f32[2048]{0:T(1024)} %param.24) | copy-start | bytes 24580
  25.8 9.5 %copy-start.25 = (f32[2,768]{1,0:T(2,128)S(1)}, f32[2,768]{1,0:T(2,128)}, u32[]{:S(2)}) copy-start(f32[2,768]{1,0:T(2,128)} %bias.1) | copy-start | bytes 18436
  25.8 207.6 %all-reduce.4.cloned.1.call-start = ((), (), s32[]{:S(2)}) async-start(), calls=%async_computation.2 | async-start | bytes 8388608 | tf_op jit(solution)/shard_map/psum | solution.py:758
  30.7 47.9 %collective-permute-start = (f32[256,2048]{1,0:T(8,128)}, f32[256,2048]{1,0:T(8,128)}, u32[]{:S(2)}, u32[]{:S(2)}) collective-permute-start(f32[256,2048]{1,0:T(8,128)} %get-tuple-element.187), channel_id=1, source_target_pairs={{0,64},{64,0},{1,65},{65,1},{2,66},{66,2},{3,67},{67,3},{4,68},{68... | collective-permute-start | bytes 6291464 | tf_op jit(solution)/shard_map/ppermute | solution.py:27
  32.7 50.0 %collective-permute-start.2 = (f32[264,2048]{1,0:T(8,128)}, f32[264,2048]{1,0:T(8,128)}, u32[]{:S(2)}, u32[]{:S(2)}) collective-permute-start(f32[264,2048]{1,0:T(8,128)} %get-tuple-element.192), channel_id=1, source_target_pairs={{0,66},{2,64},{64,2},{66,0},{1,67},{3,65},{65,3},{67,1},{4,70},{6,... | collective-permute-start | bytes 6488072 | tf_op jit(solution)/shard_map/ppermute | solution.py:734
  35.3 9.2 %copy-start.8 = (bf16[512,2048]{1,0:T(8,128)(2,1)S(1)}, bf16[512,2048]{1,0:T(8,128)(2,1)}, u32[]{:S(2)}) copy-start(bf16[512,2048]{1,0:T(8,128)(2,1)} %get-tuple-element.56.hidden) | copy-start | bytes 6291460 | tf_op jit(solution)/shard_map/cond
  58.5 8.8 %copy-start.14 = (bf16[512,2048]{1,0:T(8,128)(2,1)S(1)}, bf16[512,2048]{1,0:T(8,128)(2,1)}, u32[]{:S(2)}) copy-start(bf16[512,2048]{1,0:T(8,128)(2,1)} %get-tuple-element.82.act) | copy-start | bytes 6291460 | tf_op jit(solution)/shard_map/cond
  78.6 4.5 %collective-permute-start.1 = (f32[256,2048]{1,0:T(8,128)}, f32[256,2048]{1,0:T(8,128)}, u32[]{:S(2)}, u32[]{:S(2)}) collective-permute-start(f32[256,2048]{1,0:T(8,128)} %collective-permute-done.near), channel_id=1, source_target_pairs={{0,1},{1,0},{2,3},{3,2},{4,5},{5,4},{6,7},{7,6},{8,9},{9,8},{10,11... | collective-permute-start | bytes 6291464 | tf_op jit(solution)/shard_map/ppermute | solution.py:27
  78.7 180.4 %reduce-scatter.9.cloned.1.call-start = ((), (), s32[]{:S(2)}) async-start(), calls=%async_computation.4 | async-start | bytes 18939904
  83.1 22.7 %collective-permute-start.3 = (f32[264,2048]{1,0:T(8,128)}, f32[264,2048]{1,0:T(8,128)}, u32[]{:S(2)}, u32[]{:S(2)}) collective-permute-start(f32[264,2048]{1,0:T(8,128)} %collective-permute-done.2.near), channel_id=1, source_target_pairs={{0,1},{1,0},{2,3},{3,2},{4,5},{5,4},{6,7},{7,6},{8,9},{9,8},{10,11... | collective-permute-start | bytes 6488072 | tf_op jit(solution)/shard_map/ppermute | solution.py:27
  105.8 13.5 %copy-start.13 = (bf16[512,2048]{1,0:T(8,128)(2,1)S(1)}, bf16[512,2048]{1,0:T(8,128)(2,1)}, u32[]{:S(2)}) copy-start(bf16[512,2048]{1,0:T(8,128)(2,1)} %get-tuple-element.189.refs_9_) | copy-start | bytes 6291460
  153.1 4.4 %collective-permute-start.11 = (f32[256,2048]{1,0:T(8,128)}, f32[256,2048]{1,0:T(8,128)S(1)}, u32[]{:S(2)}, u32[]{:S(2)}) collective-permute-start(f32[256,2048]{1,0:T(8,128)} %get-tuple-element.227), channel_id=1, source_target_pairs={{0,1},{1,0},{2,3},{3,2},{4,5},{5,4},{6,7},{7,6},{8,9},{9,8},{10,11... | collective-permute-start | bytes 6291464 | tf_op jit(solution)/shard_map/ppermute | solution.py:27
  160.8 73.4 %collective-permute-start.12 = (f32[256,2048]{1,0:T(8,128)}, f32[256,2048]{1,0:T(8,128)}, u32[]{:S(2)}, u32[]{:S(2)}) collective-permute-start(f32[256,2048]{1,0:T(8,128)} %add.70), channel_id=1, source_target_pairs={{0,2},{2,0},{1,3},{3,1},{4,6},{6,4},{5,7},{7,5},{8,10},{10,8},{9,1... | collective-permute-start | bytes 6291464 | tf_op jit(solution)/shard_map/ppermute | solution.py:27
  167.3 18.4 %copy-start.17 = (f32[1,128,1792]{2,1,0:T(8,128)S(1)}, f32[1,128,1792]{2,1,0:T(8,128)}, u32[]{:S(2)}) copy-start(f32[1,128,1792]{2,1,0:T(8,128)} %reduce-scatter.7.cloned.1.call-done) | copy-start | bytes 2752516
  170.4 5.8 %collective-permute-start.4 = (f32[32,512]{1,0:T(8,128)S(1)}, f32[32,512]{1,0:T(8,128)S(1)}, u32[]{:S(2)}, u32[]{:S(2)}) collective-permute-start(f32[32,512]{1,0:T(8,128)S(1)} %concatenate.23), channel_id=1, source_target_pairs={{0,16},{16,0},{32,48},{48,32},{1,17},{17,1},{33,49},{49,33},{2,18}... | collective-permute-start | bytes 196616 | tf_op jit(solution)/shard_map/ppermute | solution.py:31
  176.2 7.6 %collective-permute-start.5 = (f32[32,512]{1,0:T(8,128)S(1)}, f32[32,512]{1,0:T(8,128)S(1)}, u32[]{:S(2)}, u32[]{:S(2)}) collective-permute-start(f32[32,512]{1,0:T(8,128)S(1)} %add.58), channel_id=1, source_target_pairs={{0,32},{16,48},{32,0},{48,16},{1,33},{17,49},{33,1},{49,17},{2,34}... | collective-permute-start | bytes 196616 | tf_op jit(solution)/shard_map/ppermute | solution.py:31
  183.8 5.1 %collective-permute-start.6 = (f32[32,512]{1,0:T(8,128)S(1)}, f32[32,512]{1,0:T(8,128)S(1)}, u32[]{:S(2)}, u32[]{:S(2)}) collective-permute-start(f32[32,512]{1,0:T(8,128)S(1)} %add.59), channel_id=1, source_target_pairs={{0,4},{4,0},{8,12},{12,8},{1,5},{5,1},{9,13},{13,9},{2,6},{6,2},{1... | collective-permute-start | bytes 196616 | tf_op jit(solution)/shard_map/ppermute | solution.py:31
  185.7 47.7 %collective-permute-start.13 = (f32[64,1792]{1,0:T(8,128)S(1)}, f32[64,1792]{1,0:T(8,128)S(1)}, u32[]{:S(2)}, u32[]{:S(2)}) collective-permute-start(f32[64,1792]{1,0:T(8,128)S(1)} %dynamic-slice_bitcast_fusion.1), channel_id=1, source_target_pairs={{0,64},{64,0},{1,65},{65,1},{2,66},{66,2},{3,67},{67,3},{4,68},{68... | collective-permute-start | bytes 1376264 | tf_op jit(solution)/shard_map/ppermute | solution.py:27
  188.9 7.9 %collective-permute-start.7 = (f32[32,512]{1,0:T(8,128)S(1)}, f32[32,512]{1,0:T(8,128)S(1)}, u32[]{:S(2)}, u32[]{:S(2)}) collective-permute-start(f32[32,512]{1,0:T(8,128)S(1)} %add.60), channel_id=1, source_target_pairs={{0,8},{4,12},{8,0},{12,4},{1,9},{5,13},{9,1},{13,5},{2,10},{6,14},... | collective-permute-start | bytes 196616 | tf_op jit(solution)/shard_map/ppermute | solution.py:31
  196.8 30.2 %collective-permute-start.8 = (f32[1,512]{1,0:T(1,128)S(1)}, f32[1,512]{1,0:T(1,128)S(1)}, u32[]{:S(2)}, u32[]{:S(2)}) collective-permute-start(f32[1,512]{1,0:T(1,128)S(1)} %constant_dynamic-slice_fusion), channel_id=1, source_target_pairs={{0,64},{64,0},{1,65},{65,1},{2,66},{66,2},{3,67},{67,3},{4,68},{68... | collective-permute-start | bytes 6152 | tf_op jit(solution)/shard_map/ppermute | solution.py:27
  227.1 1.2 collective-permute-start.9
  228.3 5.1 %collective-permute-start.10 = (f32[256]{0:T(256)S(1)}, f32[256]{0:T(256)S(1)}, u32[]{:S(2)}, u32[]{:S(2)}) collective-permute-start(f32[256]{0:T(256)S(1)} %add.68), channel_id=1, source_target_pairs={{0,2},{2,0},{1,3},{3,1},{4,6},{6,4},{5,7},{7,5},{8,10},{10,8},{9,1... | collective-permute-start | bytes 3080 | tf_op jit(solution)/shard_map/ppermute | solution.py:27
  236.8 7.8 %collective-permute-start.14 = (f32[256,2048]{1,0:T(8,128)S(1)}, f32[256,2048]{1,0:T(8,128)}, u32[]{:S(2)}, u32[]{:S(2)}) collective-permute-start(f32[256,2048]{1,0:T(8,128)S(1)} %add.72.combined), channel_id=1, source_target_pairs={{0,1},{1,0},{2,3},{3,2},{4,5},{5,4},{6,7},{7,6},{8,9},{9,8},{10,11... | collective-permute-start | bytes 6291464 | tf_op jit(solution)/shard_map/ppermute | solution.py:27
  237.7 38.0 %copy-start.29 = (f32[64]{0:T(128)}, f32[64]{0:T(128)S(1)}, u32[]{:S(2)}) copy-start(f32[64]{0:T(128)S(1)} %get-tuple-element.337) | copy-start | bytes 772
  246.3 16.2 %copy-start.19 = (f32[64,1792]{1,0:T(8,128)S(1)}, f32[64,1792]{1,0:T(8,128)}, u32[]{:S(2)}) copy-start(f32[64,1792]{1,0:T(8,128)} %copy-done.18) | copy-start | bytes 1376260
  259.1 15.3 %copy-start.2 = (f32[1,128,2176]{2,1,0:T(8,128)S(1)}, f32[1,128,2176]{2,1,0:T(8,128)}, u32[]{:S(2)}) copy-start(f32[1,128,2176]{2,1,0:T(8,128)} %reduce-scatter.9.cloned.1.call-done.near) | copy-start | bytes 3342340
  260.3 14.2 %collective-permute-start.15 = (f32[64,2176]{1,0:T(8,128)S(1)}, f32[64,2176]{1,0:T(8,128)S(1)}, u32[]{:S(2)}, u32[]{:S(2)}) collective-permute-start(f32[64,2176]{1,0:T(8,128)S(1)} %dynamic-slice_bitcast_fusion), channel_id=1, source_target_pairs={{0,64},{64,0},{1,65},{65,1},{2,66},{66,2},{3,67},{67,3},{4,68},{68... | collective-permute-start | bytes 1671176 | tf_op jit(solution)/shard_map/ppermute | solution.py:27
  (14 other events, 53.1 us)
Sparse Core Ops, SparseCore 0:
  25.8 103.9 reduce-scatter.6
  137.9 121.1 reduce-scatter.8
Sparse Core Ops, SparseCore 1:
  78.7 101.9 all-reduce.3
